TPU v7x, 512 devices: a whole 4x4x16 slice. The times are simulated.
512 devices in a mesh: section: 8 (over y, core), dp: 64 (over x, z).
Axes of the slice: x: 4, y: 4, z: 16, core: 2. Of those that a mesh axis runs over, the one named last changes fastest.
Arguments:
- update: bfloat16 [8, 128, 64, 5120], P('section', 'dp'), may hold values from -6 to 6
- outgrad: bfloat16 [8, 128, 64, 13824], P('section', 'dp'), may hold values from -6 to 6
- basis: bfloat16 [8, 5120, 128], P('section', 'dp'), may hold values from -0.078125 to 0.078125
- counts: int32 [64], replicated, may hold values from 1 to 4, as said below
Outputs:
- eigvals: float32 [8, 256, 128, 128], P('section', 'dp')
Inputs may be any that keep to these rules, and one draw needn't show every extreme that they name: counts sum to 108; owner o holds the blocks offsets[o] to offsets[o] + counts[o] - 1 in order.
All inputs are finite; a program needn't handle non-finite values.
Results may differ from a plain program's by a relative error of at most 0.0025.
Values may be sent and summed in bfloat16 or wider, within the bound.
No kernel may reach another device: no remote copies, remote signals or barrier semaphores. Data moves between devices by JAX's collectives and lax.ppermute only.
A program may use at most 128 MiB of HBM per device.

v0:
```python
import math

import jax
import jax.numpy as jnp
from jax import lax
from jax.sharding import PartitionSpec as P

FW = 13824
BLK = 128
EIG = 128


def prefix(array, axis, combine, identity):
    devices, here = (lax.axis_size(axis), lax.axis_index(axis))
    everything = lax.all_gather(array.astype(jnp.bfloat16), axis)
    start = jnp.broadcast_to(jnp.asarray(identity, array.dtype), array.shape)

    def hop(k, before):
        reached = k < here
        new = combine(before, everything[k].astype(array.dtype))
        return jnp.where(reached, new, before)

    return lax.fori_loop(0, devices, hop, start)


def add_terms(earlier, later):
    return earlier + later


def make_fold(received, length, running, portion):
    piece_rows = portion.shape[0]
    group_size = math.gcd(piece_rows, 8)
    grads_part = received
    grads_part = grads_part.reshape((piece_rows // group_size, group_size) + grads_part.shape[1:])
    rot_part = portion.reshape((piece_rows // group_size, group_size) + portion.shape[1:])

    def accumulate(summed, pair_items):
        grad_rows, rot_rows = pair_items
        project = (
            jnp.einsum("ntcb,nte->ncbe", grad_rows, rot_rows, preferred_element_type=jnp.float32)
            / length
        )
        return (summed + jnp.sum(project * project, axis=0), None)

    running, _ = lax.scan(accumulate, running, (grads_part, rot_part))
    return running


def per_device(update, outgrad, basis, counts):
    members = lax.axis_size("dp")
    own_update = update[0]
    own_float = own_update.astype(jnp.float32)
    earlier = prefix(own_float, "section", add_terms, jnp.zeros(own_float.shape, jnp.float32))
    summed = earlier + own_float
    mlp_in = summed.astype(jnp.bfloat16)
    sequences, length, features = mlp_in.shape
    flat_in = mlp_in.reshape(sequences * length, features)
    rotated = jnp.dot(
        flat_in,
        lax.all_gather(basis[0], "dp", axis=0, tiled=True),
        preferred_element_type=jnp.float32,
    )
    rotated_bf = rotated.astype(jnp.bfloat16).reshape(sequences, length, EIG)
    block_count = FW // BLK
    capacity = (2 * block_count + members - 1) // members
    offsets = jnp.cumsum(counts) - counts
    slot_range = jnp.arange(capacity, dtype=jnp.int32)
    block_index = jnp.minimum(offsets[:, None] + slot_range[None, :], block_count - 1).reshape(-1)
    slot_valid = (slot_range[None, :] < counts[:, None]).reshape(-1)
    blocks = outgrad[0].reshape(sequences, length, block_count, BLK)
    picked = jnp.take(blocks, block_index, axis=2)
    sendbuf = jnp.where(slot_valid[None, None, :, None], picked, jnp.zeros((), jnp.bfloat16))
    eigen_sum = jnp.zeros((capacity, BLK, EIG), jnp.float32)
    for micro in range(sequences):
        received = lax.all_to_all(
            sendbuf[micro : micro + 1], "dp", split_axis=2, concat_axis=0, tiled=True
        )
        eigen_sum = make_fold(
            received,
            length,
            eigen_sum,
            lax.all_gather(rotated_bf[micro : micro + 1], "dp", axis=0, tiled=True),
        )
    eigvals = eigen_sum / (sequences * members)
    return eigvals.reshape(1, capacity, BLK, EIG)


def solution(mesh):
    in_specs = (
        P("section", "dp", None, None),
        P("section", "dp", None, None),
        P("section", "dp", None),
        P(),
    )
    out_specs = P("section", "dp", None, None)
    return jax.shard_map(
        per_device, mesh=mesh, in_specs=in_specs, out_specs=out_specs, check_vma=False
    )
```

profile of v0, /device:TPU:8, one launch (start us, length us, event | category | flops | bytes accessed | tf_op | source)
XLA Modules:
  0.0 741.5 jit_solution(10794458337752626402)
XLA Ops:
  6.5 0.7 all-gather.8.cloned.1.call-update
  7.3 0.7 iota_compare_fusion
  8.0 0.7 copy.10
  8.9 0.7 sub.3
  9.9 0.1 lt.69
  10.1 6.1 reshape_squeeze.3
  16.1 2.9 copy.11
  19.1 8.7 %gather_fusion = bf16[256,2,64,128]{3,2,1,0:T(8,128)(2,1)} fusion(bf16[2,64,108,128]{3,1,2,0:T(8,128)(2,1)S(1)} %copy.11, s32[1024]{0:T(1024)S(1)} %pad_clamp_fusion), kind=kCustom, calls=%fused_computation | custom fusion | bytes 16778240 | tf_op jit(solution)/shard_map/jit(_take)/gather | solution.py:71
  27.8 5.3 select_bitcast_fusion
  33.2 3.4 fusion.16
  36.5 206.4 %all_to_all.30 = bf16[1,64,256,128]{3,1,0,2:T(8,128)(2,1)} all-to-all(bf16[1,64,256,128]{3,1,0,2:T(8,128)(2,1)S(1)} %get-tuple-element.186), channel_id=1, replica_groups=mesh['section'=8,'dp'=64] {'dp'}, dimensions={2} | all-to-all | bytes 8388608 | tf_op jit(solution)/shard_map/all_to_all | solution.py:75
  243.0 8.4 %all-to-all-start.1 = ((bf16[1,64,256,128]{3,1,0,2:T(8,128)(2,1)}), bf16[1,64,256,128]{3,1,0,2:T(8,128)(2,1)}, u32[]{:S(2)}, u32[]{:S(2)}) async-start(bf16[1,64,256,128]{3,1,0,2:T(8,128)(2,1)} %get-tuple-element.185), calls=%async_computation.1 | async-start | bytes 8388608 | tf_op jit(solution)/shard_map/all_to_all | solution.py:75
  251.4 0.7 all-gather.10.cloned.1.call-update
  252.2 22.3 %while.36 = (s32[]{:T(128)}, f32[2,64,5120]{2,1,0:T(8,128)S(1)}, s32[]{:T(128)}, bf16[8,2,64,5120]{3,2,1,0:T(8,128)(2,1)}, s32[]{:T(128)}, /*index=5*/s32[]{:T(128)}) while((s32[]{:T(128)}, f32[2,64,5120]{2,1,0:T(8,128)S(1)}, s32[]{:T(128)}, bf16[8,2,64,5120]{3,2,1,0:T(8,128)(2,1)}, s32[]{:T(128)}, /*index=5*/s32[]{:T(128)}) %tuple.64), condition=%wide.region_2.3_spmd.clone, body=%wide.region_1.2_spmd.clone.sunk | while | flops 2621444 | bytes 6553701 | solution.py:23
  252.2 2.8 add_select_fusion.2
  255.0 2.8 add_select_fusion.2
  257.8 2.8 add_select_fusion.2
  260.6 2.8 add_select_fusion.2
  263.3 2.8 add_select_fusion.2
  266.1 2.8 add_select_fusion.2
  268.9 2.8 add_select_fusion.2
  271.7 2.8 add_select_fusion.2
  274.5 2.6 fusion.10
  277.1 163.2 %all-gather.10.cloned.1.call-done = bf16[1,5120,128]{2,1,0:T(8,128)(2,1)} async-done(((bf16[1,80,128]{2,1,0:T(8,128)(2,1)}), bf16[1,5120,128]{2,1,0:T(8,128)(2,1)}) %all-gather.10.cloned.1.call-update) | async-done | bytes 1310736 | tf_op jit(solution)/shard_map/all_gather | solution.py:60
  440.4 2.2 fusion.13
  442.6 0.6 fusion.17
  443.3 0.5 all-gather.14.cloned.1.call-update
  443.8 139.1 %all-gather.12.cloned.1.call-done = bf16[4096,128]{1,0:T(8,128)(2,1)} async-done(((bf16[64,128]{1,0:T(8,128)(2,1)}), bf16[4096,128]{1,0:T(8,128)(2,1)}) %all-gather.12.cloned.1.call-update) | async-done | bytes 1048592 | tf_op jit(solution)/shard_map/all_gather | solution.py:82
  582.9 13.7 %while.37 = (s32[]{:T(128)}, f32[4,128,128]{2,1,0:T(8,128)S(1)}, bf16[8,8,64,4,128]{4,2,3,1,0:T(8,128)(2,1)}, bf16[8,8,64,128]{3,2,1,0:T(8,128)(2,1)}, s32[]{:T(128)}, /*index=5*/s32[]{:T(128)}) while((s32[]{:T(128)}, f32[4,128,128]{2,1,0:T(8,128)S(1)}, bf16[8,8,64,4,128]{4,2,3,1,0:T(8,128)(2,1)}, ...), condition=%wide.region_5.6_spmd.clone, body=%wide.region_3.5_spmd.clone.sunk | while | flops 68747264 | bytes 1705047 | solution.py:45
  582.9 1.6 multiply_reduce_fusion.5
  584.6 1.6 multiply_reduce_fusion.5
  586.3 1.6 multiply_reduce_fusion.5
  588.0 1.6 multiply_reduce_fusion.5
  589.8 1.6 multiply_reduce_fusion.5
  591.5 1.6 multiply_reduce_fusion.5
  593.2 1.6 multiply_reduce_fusion.5
  594.9 1.6 multiply_reduce_fusion.5
  596.6 124.1 %all-gather.14.cloned.1.call-done = bf16[4096,128]{1,0:T(8,128)(2,1)} async-done(((bf16[64,128]{1,0:T(8,128)(2,1)}), bf16[4096,128]{1,0:T(8,128)(2,1)}) %all-gather.14.cloned.1.call-update) | async-done | bytes 1048592 | tf_op jit(solution)/shard_map/all_gather | solution.py:82
  720.7 13.5 %while.35 = (s32[]{:T(128)}, f32[4,128,128]{2,1,0:T(8,128)S(1)}, bf16[8,8,64,4,128]{4,2,3,1,0:T(8,128)(2,1)}, bf16[8,8,64,128]{3,2,1,0:T(8,128)(2,1)}, s32[]{:T(128)}) while((s32[]{:T(128)}, f32[4,128,128]{2,1,0:T(8,128)S(1)}, bf16[8,8,64,4,128]{4,2,3,1,0:T(8,128)(2,1)}, bf16[8,8,64,128]{3,2,1,0:T(8,128)(2,1)}, s32[]{:T(128)}) %tuple.82), condition=%wide.region_8.9_spmd, body=%wide.region_6.8_spmd.sunk | while | flops 68681728 | bytes 1705029 | solution.py:45
  720.7 1.6 multiply_reduce_fusion.4
  722.4 1.6 multiply_reduce_fusion.4
  724.1 1.6 multiply_reduce_fusion.4
  725.8 1.6 multiply_reduce_fusion.4
  727.5 1.6 multiply_reduce_fusion.4
  729.2 1.6 multiply_reduce_fusion.4
  730.9 1.6 multiply_reduce_fusion.4
  732.6 1.6 multiply_reduce_fusion.4
  734.3 0.7 multiply_bitcast_fusion
  (33 shorter events, 1.8 us)
Async XLA Ops:
  6.5 245.6 %all-gather.8.cloned.1.call-start = ((), (), s32[]{:S(2)}) async-start(), calls=%async_computation.2 | async-start | bytes 11796480 | tf_op jit(solution)/shard_map/all_gather | solution.py:15
  243.0 353.6 %all-to-all-start.1 = ((bf16[1,64,256,128]{3,1,0,2:T(8,128)(2,1)}), bf16[1,64,256,128]{3,1,0,2:T(8,128)(2,1)}, u32[]{:S(2)}, u32[]{:S(2)}) async-start(bf16[1,64,256,128]{3,1,0,2:T(8,128)(2,1)} %get-tuple-element.185), calls=%async_computation.1 | async-start | bytes 8388608 | tf_op jit(solution)/shard_map/all_to_all | solution.py:75
  251.3 189.0 %all-gather.10.cloned.1.call-start = ((), (), s32[]{:S(2)}) async-start(), calls=%async_computation.3 | async-start | bytes 1331200 | tf_op jit(solution)/shard_map/all_gather | solution.py:60
  252.1 330.8 %all-gather.12.cloned.1.call-start = ((), (), s32[]{:S(2)}) async-start(), calls=%async_computation.4 | async-start | bytes 1064960 | tf_op jit(solution)/shard_map/all_gather | solution.py:82
  443.2 277.5 %all-gather.14.cloned.1.call-start = ((), (), s32[]{:S(2)}) async-start(), calls=%async_computation.5 | async-start | bytes 1064960 | tf_op jit(solution)/shard_map/all_gather | solution.py:82
Sparse Core Ops, SparseCore 0:
  9.5 69.8 all-gather.7
  255.1 185.1 all-gather.9
  443.3 139.5 all-gather.11
  585.7 134.9 all-gather.13
where the time goes:
time: 743 us; the launch traced here: 742 us
  waiting for transfers between devices  428 us (58%)
  blocking collectives  206 us (28%)
  other arithmetic  33.6 us (5%)
  matrix products  27.9 us (4%)
  local copies, waits for them, and re-layouts  22.8 us (3%)
  between operations  13.3 us (2%)
  starting transfers between devices  8.48 us (1%)
    all_gather x2, waiting for transfers between devices, per_device(): lax.all_gather(rotated_bf[micro:micro + 1], 'dp', axis=0, tiled=True)  263 us
    all_to_all x1, blocking collectives, per_device(): lax.all_to_all(sendbuf[micro:micro + 1], 'dp', split_axis=2, concat_axis=...  206 us
    all_gather x1, waiting for transfers between devices, per_device(): lax.all_gather(basis[0], 'dp', axis=0, tiled=True)  163 us
    dot_general x16, matrix products, accumulate(): jnp.einsum('ntcb,nte->ncbe', grad_rows, rot_rows, preferred_element_type=...  25.7 us
    select_n x8, other arithmetic, hop(): return jnp.where(reached, new, before)  22.1 us
  transfers between devices with their start and end apart: 5, of which 3 were waited for; matrix products, arithmetic and copies ran while one was open for 9% of the time, Pallas kernels for 0%

commit v1 on v0

v1 whole, which is shorter than its diff:
```python
import jax
import jax.numpy as jnp
from jax import lax
from jax.experimental import pallas as pl
from jax.experimental.pallas import tpu as pltpu
from jax.sharding import Mesh
from jax.sharding import PartitionSpec as P

D = 5120
FW = 13824
BLK = 128
EIG = 128
SEQ_LEN = 64
SEQS = 128
NBLK = FW // BLK
CAP = 4
N_X = 4
N_Z = 16
TOK = 128
PLANE = D // N_X
PER = 7
WID = PER * BLK
N_NEAR = 4
GROUP = N_X * N_NEAR
SECTION = ("y", "c")
DP = ("x", "z")

SMEM = pl.BlockSpec(memory_space=pltpu.SMEM)
VMEM = pl.BlockSpec(memory_space=pltpu.VMEM)


def sds(shape, dtype):
    return jax.ShapeDtypeStruct(shape, dtype)


def mod(a, n):
    return lax.rem(a + 4 * n, n)


def rotate_kernel(place, mine, other, *refs):
    bases = refs[:N_X]
    out, full = refs[N_X:]
    x, core = place[0], place[2]
    full[core] = mine[...]
    full[1 - core] = other[...]
    total = jnp.zeros((TOK, EIG), jnp.float32)
    for dx in range(N_X):
        rows = mod(x - dx, N_X)
        lane = pl.multiple_of(lax.rem(rows, 2) * PLANE, 128)
        part = full[rows // 2, :, pl.ds(lane, PLANE)]
        total = total + jnp.dot(part, bases[dx][...], preferred_element_type=jnp.float32)
    out[...] = total.T.astype(jnp.bfloat16)


def rotate(place, mine, other, bases):
    return pl.pallas_call(
        rotate_kernel,
        out_shape=sds((EIG, TOK), jnp.bfloat16),
        in_specs=[SMEM] + [VMEM] * (2 + N_X),
        out_specs=VMEM,
        scratch_shapes=[pltpu.VMEM((2, TOK, D // 2), jnp.bfloat16)],
        compiler_params=pltpu.CompilerParams(vmem_limit_bytes=32 * 2**20),
        name="rotate",
    )(place, mine, other, *bases)


def deal_kernel(counts, outgrad, out, column_of, offsets, block_of):
    def prefix(o, run):
        offsets[o] = run
        return run + counts[o]

    lax.fori_loop(0, N_X * N_Z, prefix, jnp.int32(0))

    def fill(i, _):
        column_of[i] = N_Z
        block_of[i] = 0
        return 0

    lax.fori_loop(0, 128, fill, 0)

    def owner(i, g):
        column = i // N_X
        o = lax.rem(i, N_X) * N_Z + column

        def block(s, _):
            block_of[g + s] = offsets[o] + s
            column_of[g + s] = column
            return 0

        lax.fori_loop(0, counts[o], block, 0)
        return g + counts[o]

    lax.fori_loop(0, N_X * N_Z, owner, jnp.int32(0))
    for m in range(GROUP):
        plane, member = m // N_NEAR, m % N_NEAR
        for j in range(PER):
            lane = pl.multiple_of(block_of[16 * j + 4 * member + plane] * BLK, BLK)
            for n in range(2):
                rows = slice(n * SEQ_LEN, (n + 1) * SEQ_LEN)
                out[m, rows, j * BLK : (j + 1) * BLK] = outgrad[0, n, :, pl.ds(lane, BLK)]


def deal(counts, outgrad):
    return pl.pallas_call(
        deal_kernel,
        out_shape=[sds((GROUP, TOK, WID), jnp.bfloat16), sds((128,), jnp.int32)],
        in_specs=[SMEM, VMEM],
        out_specs=[VMEM, SMEM],
        scratch_shapes=[pltpu.SMEM((N_X * N_Z,), jnp.int32), pltpu.SMEM((128,), jnp.int32)],
        compiler_params=pltpu.CompilerParams(vmem_limit_bytes=32 * 2**20),
        name="deal_blocks",
    )(counts, outgrad)


def square_kernel(place, column_of, *refs):
    rots, grad = refs[:N_X], refs[N_X]
    out, lhs, acc = refs[N_X + 1 :]
    x, member = place[0], place[3]
    lane = lax.broadcasted_iota(jnp.int32, (EIG, TOK), 1)
    zero = jnp.zeros((EIG, TOK), jnp.bfloat16)
    for dx in range(N_X):
        for k in range(N_NEAR):
            m = N_NEAR * mod(x - dx, N_X) + mod(member - k, N_NEAR)
            rot = rots[dx][k]
            lhs[m, :EIG, :] = jnp.where(lane < SEQ_LEN, rot, zero)
            lhs[m, EIG:, :] = jnp.where(lane < SEQ_LEN, zero, rot)
    for lo in range(0, WID, 256):
        hi = min(lo + 256, WID)

        def step(i, run):
            made = jnp.dot(lhs[i], grad[i, :, lo:hi], preferred_element_type=jnp.float32)
            return run + (made[:EIG] * made[:EIG] + made[EIG:] * made[EIG:])

        acc[:, lo:hi] = lax.fori_loop(0, GROUP, step, jnp.zeros((EIG, hi - lo), jnp.float32), unroll=4)
    out[...] = jnp.zeros(out.shape, out.dtype)
    first = 4 * member + x
    for j in range(PER):
        column = column_of[16 * j + first]

        @pl.when(column < N_Z)
        def _():
            out[column] = acc[:, j * BLK : (j + 1) * BLK].astype(out.dtype)


def square(place, column_of, rots, grads):
    return pl.pallas_call(
        square_kernel,
        out_shape=sds((N_Z, EIG, BLK), jnp.bfloat16),
        in_specs=[SMEM, SMEM] + [VMEM] * (N_X + 1),
        out_specs=VMEM,
        scratch_shapes=[
            pltpu.VMEM((GROUP, 2 * EIG, TOK), jnp.bfloat16),
            pltpu.VMEM((EIG, WID), jnp.float32),
        ],
        compiler_params=pltpu.CompilerParams(vmem_limit_bytes=32 * 2**20),
        name="square_sums",
    )(place, column_of, *rots, grads)


def column_starts(counts, z):
    def add(o, run):
        return run + jnp.where(lax.rem(o, N_Z) < z, counts[o], 0)

    start = lax.fori_loop(0, N_X * N_Z, add, jnp.int32(0))
    starts = []
    for k in range(N_X):
        starts.append(start)
        start = start + counts[k * N_Z + z]
    return starts


def gather_kernel(place, counts, got, out):
    x, z, core = place[0], place[1], place[2]
    for k, start in enumerate(column_starts(counts, z)):
        g = start + mod(x - start + 128, N_X)
        member = lax.rem(g // 4 + 2 * core, N_NEAR)
        owned = g < start + counts[k * N_Z + z]

        @pl.when(owned)
        def _():
            total = got[member].astype(jnp.float32)
            for far in range(4, N_Z, 4):
                total = total + got[member + far].astype(jnp.float32)
            out[k] = total

        @pl.when(jnp.logical_not(owned))
        def _():
            out[k] = jnp.zeros((EIG, BLK), jnp.float32)


def gather_nodes(place, counts, got):
    return pl.pallas_call(
        gather_kernel,
        out_shape=sds((N_X, EIG, BLK), jnp.float32),
        in_specs=[SMEM, SMEM, VMEM],
        out_specs=VMEM,
        name="gather_nodes",
    )(place, counts, got)


def finish_kernel(place, counts, got, out):
    x, z = place[0], place[1]
    starts = column_starts(counts, z)
    start = jnp.int32(0)
    for k in range(N_X):
        start = start + jnp.where(x == k, starts[k], 0)
    owned = counts[x * N_Z + z]
    scale = 1.0 / (SEQ_LEN * SEQ_LEN * SEQS)
    for s in range(CAP):
        plane = lax.rem(start + s, N_X)
        out[0, s] = jnp.where(s < owned, got[plane].T * scale, 0.0)


def finish(place, counts, got):
    return pl.pallas_call(
        finish_kernel,
        out_shape=sds((1, CAP, BLK, EIG), jnp.float32),
        in_specs=[SMEM, SMEM, VMEM],
        out_specs=VMEM,
        name="finish",
    )(place, counts, got)


def group_line(core, start):
    return [(start + 2 * core + r) % N_Z for r in range(N_NEAR)]


def index(y, core, x, z):
    return ((2 * y + core) * N_X + x) * N_Z + z


def group_exchange(v):
    groups = [
        [index(y, c, x, z) for x in range(N_X) for z in group_line(c, start)]
        for y in range(4)
        for c in range(2)
        for start in range(0, N_Z, N_NEAR)
    ]
    return lax.all_to_all(v, SECTION + DP, 0, 0, axis_index_groups=groups, tiled=True)


def group_share(v):
    line = [v]
    for k in range(1, N_NEAR):
        perm = [
            (c * N_Z + zs[r], c * N_Z + zs[(r + k) % N_NEAR])
            for c in range(2)
            for start in range(0, N_Z, N_NEAR)
            for zs in [group_line(c, start)]
            for r in range(N_NEAR)
        ]
        line.append(lax.ppermute(v, ("c", "z"), perm))
    line = jnp.stack(line)
    return [shift(line, "x", dx) for dx in range(N_X)]


def shift(v, axis, k):
    n = lax.axis_size(axis)
    return v if k == 0 else lax.ppermute(v, axis, [(i, (i + k) % n) for i in range(n)])


def stream(update):
    core = lax.axis_index("c")
    own = update[0].reshape(TOK, D)
    mine = lax.dynamic_slice_in_dim(own, core * (D // 2), D // 2, 1)
    theirs = shift(lax.dynamic_slice_in_dim(own, (1 - core) * (D // 2), D // 2, 1), "c", 1)
    mine, theirs = mine.astype(jnp.float32), theirs.astype(jnp.float32)
    pair = (mine + theirs).astype(jnp.bfloat16)
    steps = [lax.ppermute(pair, "y", [(i, i + k) for i in range(4 - k)]) for k in range(1, 4)]
    before = steps[0].astype(jnp.float32) + steps[1].astype(jnp.float32) + steps[2].astype(jnp.float32)
    low = before + jnp.where(core == 0, mine, theirs)
    high = low + jnp.where(core == 0, theirs, mine)
    low, high = low.astype(jnp.bfloat16), high.astype(jnp.bfloat16)
    return jnp.where(core == 0, low, high), shift(jnp.where(core == 0, high, low), "c", 1)


def per_device(update, outgrad, basis, counts):
    x, z, core = lax.axis_index("x"), lax.axis_index("z"), lax.axis_index("c")
    place = jnp.stack([x, z, core, (z + 2 * core) % N_NEAR]).astype(jnp.int32)
    dealt, column_of = deal(counts, outgrad)
    line = lax.all_to_all(jnp.broadcast_to(basis, (N_Z,) + basis.shape[1:]), "z", 0, 0, tiled=True)
    line, dealt = lax.optimization_barrier((line.reshape(PLANE, EIG), dealt))
    grads = group_exchange(dealt)
    bases = [shift(line, "x", dx) for dx in range(N_X)]
    mine, other = stream(update)
    rots = group_share(rotate(place, mine, other, bases))
    got = lax.all_to_all(square(place, column_of, rots, grads), "z", 0, 0, tiled=True)
    got = lax.all_to_all(gather_nodes(place, counts, got), "x", 0, 0, tiled=True)
    return finish(place, counts, got)


def solution(mesh):
    fine = Mesh(mesh.devices.reshape(4, 2, N_X, N_Z), SECTION + DP)
    return jax.shard_map(
        per_device,
        mesh=fine,
        in_specs=(P(SECTION, DP, None, None), P(SECTION, DP, None, None), P(SECTION, DP, None), P()),
        out_specs=P(SECTION, DP, None, None),
        check_vma=False,
    )
```

time: 743 us -> 188 us (0.25)
  the two profiles are of different devices: /device:TPU:8 before, /device:TPU:24 now
where the time goes in v1:
time: 188 us; the launch traced here: 187 us
  starting transfers between devices  61.6 us (33%)
  waiting for transfers between devices  53 us (28%)
  blocking collectives  46.3 us (25%)
  Pallas kernels  17.5 us (9%)
  local copies, waits for them, and re-layouts  5.96 us (3%)
  other arithmetic  2.44 us (1%)
    all_to_all x1, blocking collectives, per_device(): lax.all_to_all(square(place, column_of, rots, grads), 'z', 0, 0, tiled=True)  35.6 us
    ppermute x8, starting transfers between devices, shift(): lax.ppermute(v, axis, [(i, (i + k) % n) for i in range(n)])  26.5 us
    ppermute x8, waiting for transfers between devices, shift(): lax.ppermute(v, axis, [(i, (i + k) % n) for i in range(n)])  19.9 us
    ppermute x3, waiting for transfers between devices, stream(): lax.ppermute(pair, 'y', [(i, i + k) for i in range(4 - k)])  18.3 us
    all_to_all x1, starting transfers between devices, per_device(): lax.all_to_all(jnp.broadcast_to(basis, (N_Z,) + basis.shape[1:]), 'z', 0,...  15.2 us
    all_to_all x1, waiting for transfers between devices, per_device(): lax.all_to_all(jnp.broadcast_to(basis, (N_Z,) + basis.shape[1:]), 'z', 0,...  11.3 us
    all_to_all x1, blocking collectives, per_device(): lax.all_to_all(gather_nodes(place, counts, got), 'x', 0, 0, tiled=True)  10.8 us
    ppermute x3, starting transfers between devices, group_share(): line.append(lax.ppermute(v, ('c', 'z'), perm))  9.03 us
  transfers between devices with their start and end apart: 16, of which 10 were waited for; matrix products, arithmetic and copies ran while one was open for 1% of the time, Pallas kernels for 3%

profile of v1, /device:TPU:24, one launch (start us, length us, event | category | flops | bytes accessed | tf_op | source)
XLA Modules:
  0.0 187.1 jit_solution(16922123922302909939)
XLA Ops:
  0.0 1.5 broadcast_in_dim.8
  1.5 15.2 %all-to-all-start = ((bf16[16,80,128]{2,1,0:T(8,128)(2,1)}), bf16[16,80,128]{2,1,0:T(8,128)(2,1)S(1)}, u32[]{:S(2)}, u32[]{:S(2)}) async-start(bf16[16,80,128]{2,1,0:T(8,128)(2,1)} %broadcast_in_dim.8), calls=%async_computation | async-start | bytes 655360 | tf_op jit(solution)/shard_map/all_to_all | solution.py:281
  16.7 0.0 copy-start.1
  16.7 2.0 %copy-done.1 = bf16[1,2,64,13824]{3,2,1,0:T(8,128)(2,1)S(1)} copy-done((bf16[1,2,64,13824]{3,2,1,0:T(8,128)(2,1)S(1)}, bf16[1,2,64,13824]{3,2,1,0:T(8,128)(2,1)}, u32[]{:S(2)}) %copy-start.1) | copy-done | bytes 3538968
  18.7 0.7 copy-done.3
  19.3 5.0 %deal_blocks.1 = (bf16[16,128,896]{2,1,0:T(8,128)(2,1)S(1)}, s32[128]{0:T(128)S(1)}) custom-call(s32[64]{0:T(128)S(1)} %copy-done.3, bf16[1,2,64,13824]{3,2,1,0:T(8,128)(2,1)S(1)} %copy-done.1), custom_call_target="tpu_custom_call" | custom-call | tf_op jit(solution)/shard_map/deal_blocks/pallas_call | solution.py:104
  24.4 1.8 copy-done
  26.1 11.3 %all-to-all-done = bf16[16,80,128]{2,1,0:T(8,128)(2,1)S(1)} async-done(((bf16[16,80,128]{2,1,0:T(8,128)(2,1)}), bf16[16,80,128]{2,1,0:T(8,128)(2,1)S(1)}, u32[]{:S(2)}, u32[]{:S(2)}) %all-to-all-start) | async-done | bytes 327712 | tf_op jit(solution)/shard_map/all_to_all | solution.py:281
  37.5 7.0 %all-to-all-start.1 = ((bf16[16,128,896]{2,1,0:T(8,128)(2,1)}), bf16[16,128,896]{2,1,0:T(8,128)(2,1)}, u32[]{:S(2)}, u32[]{:S(2)}) async-start(bf16[16,128,896]{2,1,0:T(8,128)(2,1)} %copy-done), calls=%async_computation.1 | async-start | bytes 7340032 | tf_op jit(solution)/shard_map/all_to_all | solution.py:239
  44.5 1.9 %collective-permute-start = (bf16[128,2560]{1,0:T(8,128)(2,1)S(1)}, bf16[128,2560]{1,0:T(8,128)(2,1)S(1)}, u32[]{:S(2)}, u32[]{:S(2)}) collective-permute-start(bf16[128,2560]{1,0:T(8,128)(2,1)S(1)} %constant_dynamic-slice_fusion), channel_id=1, source_target_pairs={{0,64},{64,0},{1,65},{65,1},{2,66},{66,2},{3,67},{67,3},{4,68},{68... | collective-permute-start | bytes 1966088 | tf_op jit(solution)/shard_map/ppermute | solution.py:259
  46.5 2.1 %collective-permute-done = bf16[128,2560]{1,0:T(8,128)(2,1)S(1)} collective-permute-done((bf16[128,2560]{1,0:T(8,128)(2,1)S(1)}, bf16[128,2560]{1,0:T(8,128)(2,1)S(1)}, u32[]{:S(2)}, u32[]{:S(2)}) %collective-permute-start) | collective-permute-done | bytes 655392 | tf_op jit(solution)/shard_map/ppermute | solution.py:259
  48.5 0.2 fusion
  48.7 1.3 collective-permute-start.1
  50.0 1.3 collective-permute-start.2
  51.3 1.3 collective-permute-start.3
  52.6 0.1 pad_add_fusion.place
  52.7 3.8 %collective-permute-start.5 = (bf16[1280,128]{1,0:T(8,128)(2,1)S(1)}, bf16[1280,128]{1,0:T(8,128)(2,1)S(1)}, u32[]{:S(2)}, u32[]{:S(2)}) collective-permute-start(bf16[1280,128]{1,0:T(8,128)(2,1)S(1)} %bitcast.11), channel_id=1, source_target_pairs={{0,16},{16,32},{32,48},{48,0},{1,17},{17,33},{33,49},{49,1},{2,18}... | collective-permute-start | bytes 983048 | tf_op jit(solution)/shard_map/ppermute | solution.py:259
  56.5 4.6 %collective-permute-start.6 = (bf16[1280,128]{1,0:T(8,128)(2,1)S(1)}, bf16[1280,128]{1,0:T(8,128)(2,1)S(1)}, u32[]{:S(2)}, u32[]{:S(2)}) collective-permute-start(bf16[1280,128]{1,0:T(8,128)(2,1)S(1)} %bitcast.12), channel_id=1, source_target_pairs={{0,32},{16,48},{32,0},{48,16},{1,33},{17,49},{33,1},{49,17},{2,34}... | collective-permute-start | bytes 983048 | tf_op jit(solution)/shard_map/ppermute | solution.py:259
  61.1 6.4 %collective-permute-done.1 = bf16[128,2560]{1,0:T(8,128)(2,1)} collective-permute-done((bf16[128,2560]{1,0:T(8,128)(2,1)S(1)}, bf16[128,2560]{1,0:T(8,128)(2,1)}, u32[]{:S(2)}, u32[]{:S(2)}) %collective-permute-start.1) | collective-permute-done | bytes 655392 | tf_op jit(solution)/shard_map/ppermute | solution.py:269
  67.5 5.0 %collective-permute-start.7 = (bf16[1280,128]{1,0:T(8,128)(2,1)S(1)}, bf16[1280,128]{1,0:T(8,128)(2,1)S(1)}, u32[]{:S(2)}, u32[]{:S(2)}) collective-permute-start(bf16[1280,128]{1,0:T(8,128)(2,1)S(1)} %bitcast.13), channel_id=1, source_target_pairs={{0,48},{16,0},{32,16},{48,32},{1,49},{17,1},{33,17},{49,33},{2,50}... | collective-permute-start | bytes 983048 | tf_op jit(solution)/shard_map/ppermute | solution.py:259
  72.5 0.0 collective-permute-done.2
  72.5 11.8 %collective-permute-done.3 = bf16[128,2560]{1,0:T(8,128)(2,1)} collective-permute-done((bf16[128,2560]{1,0:T(8,128)(2,1)S(1)}, bf16[128,2560]{1,0:T(8,128)(2,1)}, u32[]{:S(2)}, u32[]{:S(2)}) %collective-permute-start.3) | collective-permute-done | bytes 655392 | tf_op jit(solution)/shard_map/ppermute | solution.py:269
  84.3 2.1 %broadcast_select_fusion = (bf16[128,2560]{1,0:T(8,128)(2,1)S(1)}, bf16[128,2560]{1,0:T(8,128)(2,1)S(1)}, bf16[128,2560]{1,0:T(8,128)(2,1)S(1)}) fusion(pred[]{:T(512)S(6)} %eq.4, bf16[128,2560]{1,0:T(8,128)(2,1)S(1)} %collective-permute-done, bf16[128,5120]{1,0:T(8,128)(2,1)S(1)} %bitcast.18, s32[]{:T(128)S(6)} %select_n.37, ...), kind=kLoop, calls=%fused_computation.8 | loop fusion | flops 4587520 | bytes 5242885 | tf_op jit(solution)/shard_map/jit(_where)/select_n | solution.py:274
  86.5 1.9 %collective-permute-start.4 = (bf16[128,2560]{1,0:T(8,128)(2,1)S(1)}, bf16[128,2560]{1,0:T(8,128)(2,1)S(1)}, u32[]{:S(2)}, u32[]{:S(2)}) collective-permute-start(bf16[128,2560]{1,0:T(8,128)(2,1)S(1)} %get-tuple-element.13), channel_id=1, source_target_pairs={{0,64},{64,0},{1,65},{65,1},{2,66},{66,2},{3,67},{67,3},{4,68},{68... | collective-permute-start | bytes 1966088 | tf_op jit(solution)/shard_map/ppermute | solution.py:259
  88.4 0.1 broadcast_select_fusion.1.mine
  88.5 3.5 %collective-permute-done.5.refs_1_ = bf16[1280,128]{1,0:T(8,128)(2,1)S(1)} collective-permute-done((bf16[1280,128]{1,0:T(8,128)(2,1)S(1)}, bf16[1280,128]{1,0:T(8,128)(2,1)S(1)}, u32[]{:S(2)}, u32[]{:S(2)}) %collective-permute-start.5) | collective-permute-done | bytes 327712 | tf_op jit(solution)/shard_map/ppermute | solution.py:259
  92.0 9.9 %collective-permute-done.6.refs_2_ = bf16[1280,128]{1,0:T(8,128)(2,1)S(1)} collective-permute-done((bf16[1280,128]{1,0:T(8,128)(2,1)S(1)}, bf16[1280,128]{1,0:T(8,128)(2,1)S(1)}, u32[]{:S(2)}, u32[]{:S(2)}) %collective-permute-start.6) | collective-permute-done | bytes 327712 | tf_op jit(solution)/shard_map/ppermute | solution.py:259
  101.9 0.0 collective-permute-done.7.refs_3_
  101.9 0.0 collective-permute-done.4.other
  101.9 1.2 rotate.1
  103.1 1.9 %collective-permute-start.10 = (bf16[128,128]{1,0:T(8,128)(2,1)S(1)}, bf16[128,128]{1,0:T(8,128)(2,1)S(1)}, u32[]{:S(2)}, u32[]{:S(2)}) collective-permute-start(bf16[128,128]{1,0:T(8,128)(2,1)S(1)} %rotate.1), channel_id=1, source_target_pairs={{0,3},{1,0},{2,1},{3,2},{4,7},{5,4},{6,5},{7,6},{8,11},{9,8},{10,9... | collective-permute-start | bytes 98312 | tf_op jit(solution)/shard_map/ppermute | solution.py:252
  105.0 3.9 %collective-permute-start.8 = (bf16[128,128]{1,0:T(8,128)(2,1)S(1)}, bf16[128,128]{1,0:T(8,128)(2,1)S(1)}, u32[]{:S(2)}, u32[]{:S(2)}) collective-permute-start(bf16[128,128]{1,0:T(8,128)(2,1)S(1)} %rotate.1), channel_id=1, source_target_pairs={{0,1},{1,2},{2,3},{3,0},{4,5},{5,6},{6,7},{7,4},{8,9},{9,10},{10,1... | collective-permute-start | bytes 98312 | tf_op jit(solution)/shard_map/ppermute | solution.py:252
  109.0 3.2 %collective-permute-start.9 = (bf16[128,128]{1,0:T(8,128)(2,1)S(1)}, bf16[128,128]{1,0:T(8,128)(2,1)S(1)}, u32[]{:S(2)}, u32[]{:S(2)}) collective-permute-start(bf16[128,128]{1,0:T(8,128)(2,1)S(1)} %rotate.1), channel_id=1, source_target_pairs={{0,2},{1,3},{2,0},{3,1},{4,6},{5,7},{6,4},{7,5},{8,10},{9,11},{10,... | collective-permute-start | bytes 98312 | tf_op jit(solution)/shard_map/ppermute | solution.py:252
  112.2 0.0 collective-permute-done.10
  112.2 0.5 collective-permute-done.8
  112.7 3.1 %collective-permute-done.9 = bf16[128,128]{1,0:T(8,128)(2,1)S(1)} collective-permute-done((bf16[128,128]{1,0:T(8,128)(2,1)S(1)}, bf16[128,128]{1,0:T(8,128)(2,1)S(1)}, u32[]{:S(2)}, u32[]{:S(2)}) %collective-permute-start.9) | collective-permute-done | bytes 32800 | tf_op jit(solution)/shard_map/ppermute | solution.py:252
  115.8 1.9 %collective-permute-start.11 = (bf16[4,128,128]{2,1,0:T(8,128)(2,1)S(1)}, bf16[4,128,128]{2,1,0:T(8,128)(2,1)S(1)}, u32[]{:S(2)}, u32[]{:S(2)}) collective-permute-start(bf16[4,128,128]{2,1,0:T(8,128)(2,1)S(1)} %pad_maximum_fusion.refs_0_), channel_id=1, source_target_pairs={{0,16},{16,32},{32,48},{48,0},{1,17},{17,33},{33,49},{49,1},{2,18}... | collective-permute-start | bytes 393224 | tf_op jit(solution)/shard_map/ppermute | solution.py:259
  117.7 2.8 %collective-permute-start.12 = (bf16[4,128,128]{2,1,0:T(8,128)(2,1)S(1)}, bf16[4,128,128]{2,1,0:T(8,128)(2,1)S(1)}, u32[]{:S(2)}, u32[]{:S(2)}) collective-permute-start(bf16[4,128,128]{2,1,0:T(8,128)(2,1)S(1)} %pad_maximum_fusion.refs_0_), channel_id=1, source_target_pairs={{0,32},{16,48},{32,0},{48,16},{1,33},{17,49},{33,1},{49,17},{2,34}... | collective-permute-start | bytes 393224 | tf_op jit(solution)/shard_map/ppermute | solution.py:259
  120.6 4.5 %collective-permute-start.13 = (bf16[4,128,128]{2,1,0:T(8,128)(2,1)S(1)}, bf16[4,128,128]{2,1,0:T(8,128)(2,1)S(1)}, u32[]{:S(2)}, u32[]{:S(2)}) collective-permute-start(bf16[4,128,128]{2,1,0:T(8,128)(2,1)S(1)} %pad_maximum_fusion.refs_0_), channel_id=1, source_target_pairs={{0,48},{16,0},{32,16},{48,32},{1,49},{17,1},{33,17},{49,33},{2,50}... | collective-permute-start | bytes 393224 | tf_op jit(solution)/shard_map/ppermute | solution.py:259
  125.1 1.6 collective-permute-done.11.refs_1_
  126.7 0.0 collective-permute-done.12.refs_2_
  126.7 2.8 %collective-permute-done.13.refs_3_ = bf16[4,128,128]{2,1,0:T(8,128)(2,1)S(1)} collective-permute-done((bf16[4,128,128]{2,1,0:T(8,128)(2,1)S(1)}, bf16[4,128,128]{2,1,0:T(8,128)(2,1)S(1)}, u32[]{:S(2)}, u32[]{:S(2)}) %collective-permute-start.13) | collective-permute-done | bytes 131104 | tf_op jit(solution)/shard_map/ppermute | solution.py:259
  129.4 0.0 all-to-all-done.1.refs_4_
  129.4 6.8 %square_sums.1 = bf16[16,128,128]{2,1,0:T(8,128)(2,1)S(1)} custom-call(s32[4]{0:T(128)S(1)} %pad_add_fusion.place, s32[128]{0:T(128)S(1)} %get-tuple-element.9.column_of, bf16[4,128,128]{2,1,0:T(8,128)(2,1)S(1)} %pad_maximum_fusion.refs_0_, bf16[4,128,128]{2,1,0:T(8,128)(2,1)S(1)} %collective-permute-done.11.refs_1_, ...), custom_call_target="tpu_custom_call" | custom-call | tf_op jit(solution)/shard_map/square_sums/pallas_call | solution.py:146
  136.2 35.6 %all_to_all.20.got = bf16[16,128,128]{2,1,0:T(8,128)(2,1)} all-to-all(bf16[16,128,128]{2,1,0:T(8,128)(2,1)S(1)} %square_sums.1), channel_id=1, replica_groups=mesh['y'=4,'c'=2,'x'=4,'z'=16] {'z'}, dimensions={0} | all-to-all | bytes 1048576 | tf_op jit(solution)/shard_map/all_to_all | solution.py:287
  171.8 2.3 %gather_nodes.1 = f32[4,128,128]{2,1,0:T(8,128)} custom-call(s32[4]{0:T(128)} %copy-done.2, s32[64]{0:T(128)} %counts.5, bf16[16,128,128]{2,1,0:T(8,128)(2,1)} %all_to_all.20.got), custom_call_target="tpu_custom_call" | custom-call | tf_op jit(solution)/shard_map/gather_nodes/pallas_call | solution.py:192
  174.1 10.8 %all_to_all.21.got = f32[4,128,128]{2,1,0:T(8,128)} all-to-all(f32[4,128,128]{2,1,0:T(8,128)} %gather_nodes.1), channel_id=1, replica_groups=mesh['y'=4,'c'=2,'x'=4,'z'=16] {'x'}, dimensions={0} | all-to-all | bytes 524288 | tf_op jit(solution)/shard_map/all_to_all | solution.py:288
  184.9 2.2 %finish.1 = f32[1,4,128,128]{3,2,1,0:T(8,128)} custom-call(s32[4]{0:T(128)} %copy-done.2, s32[64]{0:T(128)} %counts.5, f32[4,128,128]{2,1,0:T(8,128)} %all_to_all.21.got), custom_call_target="tpu_custom_call" | custom-call | tf_op jit(solution)/shard_map/finish/pallas_call | solution.py:215
  (8 shorter events, 0.1 us)
Async XLA Ops:
  1.5 36.0 %all-to-all-start = ((bf16[16,80,128]{2,1,0:T(8,128)(2,1)}), bf16[16,80,128]{2,1,0:T(8,128)(2,1)S(1)}, u32[]{:S(2)}, u32[]{:S(2)}) async-start(bf16[16,80,128]{2,1,0:T(8,128)(2,1)} %broadcast_in_dim.8), calls=%async_computation | async-start | bytes 655360 | tf_op jit(solution)/shard_map/all_to_all | solution.py:281
  16.7 2.0 %copy-start.1 = (bf16[1,2,64,13824]{3,2,1,0:T(8,128)(2,1)S(1)}, bf16[1,2,64,13824]{3,2,1,0:T(8,128)(2,1)}, u32[]{:S(2)}) copy-start(bf16[1,2,64,13824]{3,2,1,0:T(8,128)(2,1)} %outgrad.1) | copy-start | bytes 10616836
  18.7 0.7 copy-start.3
  24.3 1.8 copy-start
  37.5 7.0 %copy-start.4 = (bf16[1,2,64,5120]{3,2,1,0:T(8,128)(2,1)S(1)}, bf16[1,2,64,5120]{3,2,1,0:T(8,128)(2,1)}, u32[]{:S(2)}) copy-start(bf16[1,2,64,5120]{3,2,1,0:T(8,128)(2,1)} %param.4) | copy-start | bytes 3932164
  37.5 92.0 %all-to-all-start.1 = ((bf16[16,128,896]{2,1,0:T(8,128)(2,1)}), bf16[16,128,896]{2,1,0:T(8,128)(2,1)}, u32[]{:S(2)}, u32[]{:S(2)}) async-start(bf16[16,128,896]{2,1,0:T(8,128)(2,1)} %copy-done), calls=%async_computation.1 | async-start | bytes 7340032 | tf_op jit(solution)/shard_map/all_to_all | solution.py:239
  44.5 4.0 %collective-permute-start = (bf16[128,2560]{1,0:T(8,128)(2,1)S(1)}, bf16[128,2560]{1,0:T(8,128)(2,1)S(1)}, u32[]{:S(2)}, u32[]{:S(2)}) collective-permute-start(bf16[128,2560]{1,0:T(8,128)(2,1)S(1)} %constant_dynamic-slice_fusion), channel_id=1, source_target_pairs={{0,64},{64,0},{1,65},{65,1},{2,66},{66,2},{3,67},{67,3},{4,68},{68... | collective-permute-start | bytes 1966088 | tf_op jit(solution)/shard_map/ppermute | solution.py:259
  48.7 18.8 %collective-permute-start.1 = (bf16[128,2560]{1,0:T(8,128)(2,1)S(1)}, bf16[128,2560]{1,0:T(8,128)(2,1)}, u32[]{:S(2)}, u32[]{:S(2)}) collective-permute-start(bf16[128,2560]{1,0:T(8,128)(2,1)S(1)} %fusion), channel_id=1, source_target_pairs={{0,128},{128,256},{256,384},{1,129},{129,257},{257,385},{2,130},{1... | collective-permute-start | bytes 1966088 | tf_op jit(solution)/shard_map/ppermute | solution.py:269
  50.0 22.5 %collective-permute-start.2 = (bf16[128,2560]{1,0:T(8,128)(2,1)S(1)}, bf16[128,2560]{1,0:T(8,128)(2,1)}, u32[]{:S(2)}, u32[]{:S(2)}) collective-permute-start(bf16[128,2560]{1,0:T(8,128)(2,1)S(1)} %fusion), channel_id=1, source_target_pairs={{0,256},{128,384},{1,257},{129,385},{2,258},{130,386},{3,259},{131... | collective-permute-start | bytes 1966088 | tf_op jit(solution)/shard_map/ppermute | solution.py:269
  51.3 33.0 %collective-permute-start.3 = (bf16[128,2560]{1,0:T(8,128)(2,1)S(1)}, bf16[128,2560]{1,0:T(8,128)(2,1)}, u32[]{:S(2)}, u32[]{:S(2)}) collective-permute-start(bf16[128,2560]{1,0:T(8,128)(2,1)S(1)} %fusion), channel_id=1, source_target_pairs={{0,384},{1,385},{2,386},{3,387},{4,388},{5,389},{6,390},{7,391},{8... | collective-permute-start | bytes 1966088 | tf_op jit(solution)/shard_map/ppermute | solution.py:269
  52.7 76.7 %copy-start.2 = (s32[4]{0:T(128)}, s32[4]{0:T(128)S(1)}, u32[]{:S(2)}) copy-start(s32[4]{0:T(128)S(1)} %pad_add_fusion.place) | copy-start | bytes 52
  52.7 39.3 %collective-permute-start.5 = (bf16[1280,128]{1,0:T(8,128)(2,1)S(1)}, bf16[1280,128]{1,0:T(8,128)(2,1)S(1)}, u32[]{:S(2)}, u32[]{:S(2)}) collective-permute-start(bf16[1280,128]{1,0:T(8,128)(2,1)S(1)} %bitcast.11), channel_id=1, source_target_pairs={{0,16},{16,32},{32,48},{48,0},{1,17},{17,33},{33,49},{49,1},{2,18}... | collective-permute-start | bytes 983048 | tf_op jit(solution)/shard_map/ppermute | solution.py:259
  56.5 45.5 %collective-permute-start.6 = (bf16[1280,128]{1,0:T(8,128)(2,1)S(1)}, bf16[1280,128]{1,0:T(8,128)(2,1)S(1)}, u32[]{:S(2)}, u32[]{:S(2)}) collective-permute-start(bf16[1280,128]{1,0:T(8,128)(2,1)S(1)} %bitcast.12), channel_id=1, source_target_pairs={{0,32},{16,48},{32,0},{48,16},{1,33},{17,49},{33,1},{49,17},{2,34}... | collective-permute-start | bytes 983048 | tf_op jit(solution)/shard_map/ppermute | solution.py:259
  67.5 34.4 %collective-permute-start.7 = (bf16[1280,128]{1,0:T(8,128)(2,1)S(1)}, bf16[1280,128]{1,0:T(8,128)(2,1)S(1)}, u32[]{:S(2)}, u32[]{:S(2)}) collective-permute-start(bf16[1280,128]{1,0:T(8,128)(2,1)S(1)} %bitcast.13), channel_id=1, source_target_pairs={{0,48},{16,0},{32,16},{48,32},{1,49},{17,1},{33,17},{49,33},{2,50}... | collective-permute-start | bytes 983048 | tf_op jit(solution)/shard_map/ppermute | solution.py:259
  86.5 15.5 %collective-permute-start.4 = (bf16[128,2560]{1,0:T(8,128)(2,1)S(1)}, bf16[128,2560]{1,0:T(8,128)(2,1)S(1)}, u32[]{:S(2)}, u32[]{:S(2)}) collective-permute-start(bf16[128,2560]{1,0:T(8,128)(2,1)S(1)} %get-tuple-element.13), channel_id=1, source_target_pairs={{0,64},{64,0},{1,65},{65,1},{2,66},{66,2},{3,67},{67,3},{4,68},{68... | collective-permute-start | bytes 1966088 | tf_op jit(solution)/shard_map/ppermute | solution.py:259
  103.1 9.1 %collective-permute-start.10 = (bf16[128,128]{1,0:T(8,128)(2,1)S(1)}, bf16[128,128]{1,0:T(8,128)(2,1)S(1)}, u32[]{:S(2)}, u32[]{:S(2)}) collective-permute-start(bf16[128,128]{1,0:T(8,128)(2,1)S(1)} %rotate.1), channel_id=1, source_target_pairs={{0,3},{1,0},{2,1},{3,2},{4,7},{5,4},{6,5},{7,6},{8,11},{9,8},{10,9... | collective-permute-start | bytes 98312 | tf_op jit(solution)/shard_map/ppermute | solution.py:252
  105.0 7.6 %collective-permute-start.8 = (bf16[128,128]{1,0:T(8,128)(2,1)S(1)}, bf16[128,128]{1,0:T(8,128)(2,1)S(1)}, u32[]{:S(2)}, u32[]{:S(2)}) collective-permute-start(bf16[128,128]{1,0:T(8,128)(2,1)S(1)} %rotate.1), channel_id=1, source_target_pairs={{0,1},{1,2},{2,3},{3,0},{4,5},{5,6},{6,7},{7,4},{8,9},{9,10},{10,1... | collective-permute-start | bytes 98312 | tf_op jit(solution)/shard_map/ppermute | solution.py:252
  109.0 6.8 %collective-permute-start.9 = (bf16[128,128]{1,0:T(8,128)(2,1)S(1)}, bf16[128,128]{1,0:T(8,128)(2,1)S(1)}, u32[]{:S(2)}, u32[]{:S(2)}) collective-permute-start(bf16[128,128]{1,0:T(8,128)(2,1)S(1)} %rotate.1), channel_id=1, source_target_pairs={{0,2},{1,3},{2,0},{3,1},{4,6},{5,7},{6,4},{7,5},{8,10},{9,11},{10,... | collective-permute-start | bytes 98312 | tf_op jit(solution)/shard_map/ppermute | solution.py:252
  115.8 10.9 %collective-permute-start.11 = (bf16[4,128,128]{2,1,0:T(8,128)(2,1)S(1)}, bf16[4,128,128]{2,1,0:T(8,128)(2,1)S(1)}, u32[]{:S(2)}, u32[]{:S(2)}) collective-permute-start(bf16[4,128,128]{2,1,0:T(8,128)(2,1)S(1)} %pad_maximum_fusion.refs_0_), channel_id=1, source_target_pairs={{0,16},{16,32},{32,48},{48,0},{1,17},{17,33},{33,49},{49,1},{2,18}... | collective-permute-start | bytes 393224 | tf_op jit(solution)/shard_map/ppermute | solution.py:259
  117.7 9.0 %collective-permute-start.12 = (bf16[4,128,128]{2,1,0:T(8,128)(2,1)S(1)}, bf16[4,128,128]{2,1,0:T(8,128)(2,1)S(1)}, u32[]{:S(2)}, u32[]{:S(2)}) collective-permute-start(bf16[4,128,128]{2,1,0:T(8,128)(2,1)S(1)} %pad_maximum_fusion.refs_0_), channel_id=1, source_target_pairs={{0,32},{16,48},{32,0},{48,16},{1,33},{17,49},{33,1},{49,17},{2,34}... | collective-permute-start | bytes 393224 | tf_op jit(solution)/shard_map/ppermute | solution.py:259
  120.6 8.9 %collective-permute-start.13 = (bf16[4,128,128]{2,1,0:T(8,128)(2,1)S(1)}, bf16[4,128,128]{2,1,0:T(8,128)(2,1)S(1)}, u32[]{:S(2)}, u32[]{:S(2)}) collective-permute-start(bf16[4,128,128]{2,1,0:T(8,128)(2,1)S(1)} %pad_maximum_fusion.refs_0_), channel_id=1, source_target_pairs={{0,48},{16,0},{32,16},{48,32},{1,49},{17,1},{33,17},{49,33},{2,50}... | collective-permute-start | bytes 393224 | tf_op jit(solution)/shard_map/ppermute | solution.py:259

commit v2 on v1

v2 whole, which is shorter than its diff:
```python
import jax
import jax.numpy as jnp
from jax import lax
from jax.experimental import pallas as pl
from jax.experimental.pallas import tpu as pltpu
from jax.sharding import Mesh
from jax.sharding import PartitionSpec as P

D = 5120
FW = 13824
BLK = 128
EIG = 128
SEQ_LEN = 64
SEQS = 128
NBLK = FW // BLK
CAP = 4
N_X = 4
N_Z = 16
TOK = 128
PLANE = D // N_X
SLOTS = 56
WID = SLOTS * BLK
PER = 7
GROUP = 8
SECTION = ("y", "c")
DP = ("x", "z")

SMEM = pl.BlockSpec(memory_space=pltpu.SMEM)
VMEM = pl.BlockSpec(memory_space=pltpu.VMEM)


def sds(shape, dtype):
    return jax.ShapeDtypeStruct(shape, dtype)


def mod(a, n):
    return lax.rem(a + 4 * n, n)


def rotate_kernel(place, mine, other, *refs):
    bases = refs[:N_X]
    out, full = refs[N_X:]
    x, core = place[0], place[2]
    full[core] = mine[...]
    full[1 - core] = other[...]
    total = jnp.zeros((TOK, EIG), jnp.float32)
    for dx in range(N_X):
        rows = mod(x - dx, N_X)
        lane = pl.multiple_of(lax.rem(rows, 2) * PLANE, 128)
        part = full[rows // 2, :, pl.ds(lane, PLANE)]
        total = total + jnp.dot(part, bases[dx][...], preferred_element_type=jnp.float32)
    out[...] = total.T.astype(jnp.bfloat16)


def rotate(place, mine, other, bases):
    return pl.pallas_call(
        rotate_kernel,
        out_shape=sds((EIG, TOK), jnp.bfloat16),
        in_specs=[SMEM] + [VMEM] * (2 + N_X),
        out_specs=VMEM,
        scratch_shapes=[pltpu.VMEM((2, TOK, D // 2), jnp.bfloat16)],
        compiler_params=pltpu.CompilerParams(vmem_limit_bytes=32 * 2**20),
        name="rotate",
    )(place, mine, other, *bases)


def deal_kernel(place, counts, outgrad, kept, sent_up, sent_down, column_of, starts, offsets, block_of):
    z = place[1]

    def prefix(o, run):
        offsets[o] = run
        return run + counts[o]

    lax.fori_loop(0, N_X * N_Z, prefix, jnp.int32(0))

    def fill(i, _):
        column_of[i] = N_Z
        block_of[i] = 0
        return 0

    lax.fori_loop(0, 128, fill, 0)

    def owner(i, g):
        column = i // N_X
        o = lax.rem(i, N_X) * N_Z + column

        @pl.when(column == z)
        def _():
            starts[lax.rem(i, N_X)] = g

        def block(s, _):
            block_of[g + s] = offsets[o] + s
            column_of[g + s] = column
            return 0

        lax.fori_loop(0, counts[o], block, 0)
        return g + counts[o]

    lax.fori_loop(0, N_X * N_Z, owner, jnp.int32(0))
    for m in range(2):
        near = lax.rem(place[3] + m, 2)
        for i in range(SLOTS):
            g = 16 * (i // 8) + 8 * (i // 4 % 2) + 4 * near + i % 4
            lane = pl.multiple_of(block_of[g] * BLK, BLK)
            for n in range(2):
                out = (kept.at[n * SEQ_LEN : (n + 1) * SEQ_LEN], (sent_up, sent_down)[n])[m]
                out[:, i * BLK : (i + 1) * BLK] = outgrad[0, n, :, pl.ds(lane, BLK)]


def deal(place, counts, outgrad):
    return pl.pallas_call(
        deal_kernel,
        out_shape=[sds((rows, WID), jnp.bfloat16) for rows in (TOK, SEQ_LEN, SEQ_LEN)] + [sds((128,), jnp.int32), sds((N_X,), jnp.int32)],
        in_specs=[SMEM, SMEM, VMEM],
        out_specs=[VMEM, VMEM, VMEM, SMEM, SMEM],
        scratch_shapes=[pltpu.SMEM((N_X * N_Z,), jnp.int32), pltpu.SMEM((128,), jnp.int32)],
        compiler_params=pltpu.CompilerParams(vmem_limit_bytes=32 * 2**20),
        name="deal_blocks",
    )(place, counts, outgrad)


def square_kernel(*refs):
    (own, up, down), (kept, got_up, got_down) = refs[:3], refs[3:6]
    out, lhs = refs[6:]
    lane = lax.broadcasted_iota(jnp.int32, (EIG, TOK), 1)
    zero = jnp.zeros((EIG, TOK), jnp.bfloat16)
    lhs[:EIG, :] = jnp.where(lane < SEQ_LEN, own[...], zero)
    lhs[EIG:, :] = jnp.where(lane < SEQ_LEN, zero, own[...])
    first, second = up[:, :SEQ_LEN], down[:, SEQ_LEN:]
    for i in range(0, SLOTS, 2):
        cols = slice(i * BLK, (i + 2) * BLK)
        made = jnp.dot(lhs[...], kept[:, cols], preferred_element_type=jnp.float32)
        made = made * made
        total = made[:EIG] + made[EIG:]
        for rot, grad in ((first, got_up), (second, got_down)):
            made = jnp.dot(rot, grad[:, cols], preferred_element_type=jnp.float32)
            total = total + made * made
        for k in range(2):
            member = 2 * ((i + k) % 4) + (i + k) // 4 % 2
            out[member, i // 8] = total[:, k * BLK : (k + 1) * BLK].astype(out.dtype)


def square(rots, grads):
    return pl.pallas_call(
        square_kernel,
        out_shape=sds((GROUP, PER, EIG, BLK), jnp.bfloat16),
        in_specs=[VMEM] * 6,
        out_specs=VMEM,
        scratch_shapes=[pltpu.VMEM((2 * EIG, TOK), jnp.bfloat16)],
        compiler_params=pltpu.CompilerParams(vmem_limit_bytes=32 * 2**20),
        name="square_sums",
    )(*rots, *grads)


def group_kernel(place, column_of, got, out):
    first = 4 * place[3] + place[0]
    out[...] = jnp.zeros(out.shape, out.dtype)
    for j in range(PER):
        column = column_of[16 * j + first]

        @pl.when(column < N_Z)
        def _():
            total = got[0, j].astype(jnp.float32)
            for r in range(1, GROUP):
                total = total + got[r, j].astype(jnp.float32)
            out[column] = total.astype(out.dtype)


def group_sums(place, column_of, got):
    return pl.pallas_call(
        group_kernel,
        out_shape=sds((N_Z, EIG, BLK), jnp.bfloat16),
        in_specs=[SMEM, SMEM, VMEM],
        out_specs=VMEM,
        name="group_sums",
    )(place, column_of, got)


def gather_kernel(place, counts, starts, got, out):
    x, z, core = place[0], place[1], place[2]
    for k in range(N_X):
        start = starts[k]
        g = start + mod(x - start + 128, N_X)
        member = lax.rem(g // 4 + 2 * core, 4)
        owned = g < start + counts[k * N_Z + z]

        @pl.when(owned)
        def _():
            total = got[member].astype(jnp.float32)
            for far in range(4, N_Z, 4):
                total = total + got[member + far].astype(jnp.float32)
            out[k] = total

        @pl.when(jnp.logical_not(owned))
        def _():
            out[k] = jnp.zeros((EIG, BLK), jnp.float32)


def gather_nodes(place, counts, starts, got):
    return pl.pallas_call(
        gather_kernel,
        out_shape=sds((N_X, EIG, BLK), jnp.float32),
        in_specs=[SMEM, SMEM, SMEM, VMEM],
        out_specs=VMEM,
        name="gather_nodes",
    )(place, counts, starts, got)


def finish_kernel(place, counts, starts, got, out):
    x, z = place[0], place[1]
    start = starts[x]
    owned = counts[x * N_Z + z]
    scale = 1.0 / (SEQ_LEN * SEQ_LEN * SEQS)
    for s in range(CAP):
        plane = lax.rem(start + s, N_X)

        @pl.when(s < owned)
        def _():
            out[0, s] = got[plane].T * scale

        @pl.when(s >= owned)
        def _():
            out[0, s] = jnp.zeros((BLK, EIG), jnp.float32)


def finish(place, counts, starts, got):
    return pl.pallas_call(
        finish_kernel,
        out_shape=sds((1, CAP, BLK, EIG), jnp.float32),
        in_specs=[SMEM, SMEM, SMEM, VMEM],
        out_specs=VMEM,
        name="finish",
    )(place, counts, starts, got)


def index(y, core, x, z):
    return ((2 * y + core) * N_X + x) * N_Z + z


def ring(core, place):
    return (place - 2 * core) % N_Z


def group_exchange(v):
    groups = [
        [index(y, c, x, ring(c, start + near + far)) for x in range(N_X) for far in (0, 2)]
        for y in range(4)
        for c in range(2)
        for start in range(0, N_Z, 4)
        for near in range(2)
    ]
    return lax.all_to_all(v, SECTION + DP, 0, 0, axis_index_groups=groups, tiled=True)


def swap(v, first):
    pairs = [(first + p, first + p + 1) for p in range(0, N_Z, 2)]
    pairs += [(b, a) for a, b in pairs]
    return lax.ppermute(v, "z", [(a % N_Z, b % N_Z) for a, b in pairs])


def shift(v, axis, k):
    n = lax.axis_size(axis)
    return v if k == 0 else lax.ppermute(v, axis, [(i, (i + k) % n) for i in range(n)])


def chip_sums(update):
    core = lax.axis_index("c")
    own = update[0].reshape(TOK, D)
    mine = lax.dynamic_slice_in_dim(own, core * (D // 2), D // 2, 1)
    theirs = shift(lax.dynamic_slice_in_dim(own, (1 - core) * (D // 2), D // 2, 1), "c", 1)
    pair = (mine.astype(jnp.float32) + theirs.astype(jnp.float32)).astype(jnp.bfloat16)
    return mine, theirs, pair, lax.ppermute(pair, "y", [(0, 1), (1, 2), (2, 3)])


def stream(mine, theirs, pair, one):
    core = lax.axis_index("c")
    mine, theirs = mine.astype(jnp.float32), theirs.astype(jnp.float32)
    two = (pair.astype(jnp.float32) + one.astype(jnp.float32)).astype(jnp.bfloat16)
    before = one.astype(jnp.float32) + lax.ppermute(two, "y", [(0, 2), (1, 3)]).astype(jnp.float32)
    low = before + jnp.where(core == 0, mine, theirs)
    high = low + jnp.where(core == 0, theirs, mine)
    low, high = low.astype(jnp.bfloat16), high.astype(jnp.bfloat16)
    return jnp.where(core == 0, low, high), shift(jnp.where(core == 0, high, low), "c", 1)


def per_device(update, outgrad, basis, counts):
    x, z, core = lax.axis_index("x"), lax.axis_index("z"), lax.axis_index("c")
    place = jnp.stack([x, z, core, (z + 2 * core) % 4]).astype(jnp.int32)
    line = lax.all_to_all(jnp.broadcast_to(basis, (N_Z,) + basis.shape[1:]), "z", 0, 0, tiled=True)
    line = line.reshape(PLANE, EIG)
    kept, up, down, column_of, starts = deal(place, counts, outgrad)
    mine, theirs, pair, one = chip_sums(update)
    grads = [kept, swap(up, 0), swap(down, 1)]
    bases = [shift(line, "x", dx) for dx in range(N_X)]
    mine, other = stream(mine, theirs, pair, one)
    rotated = rotate(place, mine, other, bases)
    rotated, grads = lax.optimization_barrier((rotated, grads))
    got = group_exchange(square([rotated, swap(rotated, 0), swap(rotated, 1)], grads))
    got = lax.all_to_all(group_sums(place, column_of, got), "z", 0, 0, tiled=True)
    got = lax.all_to_all(gather_nodes(place, counts, starts, got), "x", 0, 0, tiled=True)
    return finish(place, counts, starts, got)


def solution(mesh):
    fine = Mesh(mesh.devices.reshape(4, 2, N_X, N_Z), SECTION + DP)
    return jax.shard_map(
        per_device,
        mesh=fine,
        in_specs=(P(SECTION, DP, None, None), P(SECTION, DP, None, None), P(SECTION, DP, None), P()),
        out_specs=P(SECTION, DP, None, None),
        check_vma=False,
    )
```

time: 188 us -> 175 us (0.931)
  the two profiles are of different devices: /device:TPU:24 before, /device:TPU:32 now
where the time goes in v2:
time: 175 us; the launch traced here: 174 us
  blocking collectives  78.4 us (45%)
  starting transfers between devices  56 us (32%)
  Pallas kernels  15.9 us (9%)
  waiting for transfers between devices  12.8 us (7%)
  other arithmetic  7.05 us (4%)
  local copies, waits for them, and re-layouts  3.9 us (2%)
    all_to_all x1, blocking collectives, per_device(): lax.all_to_all(group_sums(place, column_of, got), 'z', 0, 0, tiled=True)  40.9 us
    all_to_all x1, blocking collectives, group_exchange(): lax.all_to_all(v, SECTION + DP, 0, 0, axis_index_groups=groups, tiled=True)  26.8 us
    ppermute x4, starting transfers between devices, swap(): return lax.ppermute(v, 'z', [(a % N_Z, b % N_Z) for a, b in pairs])  17.5 us
    all_to_all x1, starting transfers between devices, per_device(): lax.all_to_all(jnp.broadcast_to(basis, (N_Z,) + basis.shape[1:]), 'z', 0,...  15.3 us
    ppermute x5, starting transfers between devices, shift(): lax.ppermute(v, axis, [(i, (i + k) % n) for i in range(n)])  14 us
    ppermute x5, waiting for transfers between devices, shift(): lax.ppermute(v, axis, [(i, (i + k) % n) for i in range(n)])  10.9 us
    all_to_all x1, blocking collectives, per_device(): lax.all_to_all(gather_nodes(place, counts, starts, got), 'x', 0, 0, tiled...  10.8 us
    pallas_call x1, Pallas kernels, deal(): pl.pallas_call(deal_kernel, out_shape=[sds((rows, WID), jnp.bfloat16) for...  5.94 us
  transfers between devices with their start and end apart: 12, of which 4 were waited for; matrix products, arithmetic and copies ran while one was open for 4% of the time, Pallas kernels for 4%

profile of v2, /device:TPU:32, one launch (start us, length us, event | category | flops | bytes accessed | tf_op | source)
XLA Modules:
  0.0 174.3 jit_solution(9610623425840569632)
XLA Ops:
  0.0 1.1 constant_dynamic-slice_fusion
  1.1 1.9 %collective-permute-start = (bf16[128,2560]{1,0:T(8,128)(2,1)S(1)}, bf16[128,2560]{1,0:T(8,128)(2,1)}, u32[]{:S(2)}, u32[]{:S(2)}) collective-permute-start(bf16[128,2560]{1,0:T(8,128)(2,1)S(1)} %constant_dynamic-slice_fusion), channel_id=1, source_target_pairs={{0,64},{64,0},{1,65},{65,1},{2,66},{66,2},{3,67},{67,3},{4,68},{68... | collective-permute-start | bytes 1966088 | tf_op jit(solution)/shard_map/ppermute | solution.py:263
  3.1 2.2 %collective-permute-done = bf16[128,2560]{1,0:T(8,128)(2,1)} collective-permute-done((bf16[128,2560]{1,0:T(8,128)(2,1)S(1)}, bf16[128,2560]{1,0:T(8,128)(2,1)}, u32[]{:S(2)}, u32[]{:S(2)}) %collective-permute-start) | collective-permute-done | bytes 655392 | tf_op jit(solution)/shard_map/ppermute | solution.py:263
  5.3 2.4 %fusion.2 = bf16[128,2560]{1,0:T(8,128)(2,1)} fusion(bf16[128,2560]{1,0:T(8,128)(2,1)} %collective-permute-done, bf16[128,5120]{1,0:T(8,128)(2,1)} %bitcast.8, s32[]{:T(128)S(6)} %select_n.37), kind=kLoop, calls=%fused_computation.7 | loop fusion | flops 1310720 | bytes 1966084 | tf_op jit(solution)/shard_map/convert_element_type | solution.py:271
  7.7 4.3 %collective-permute-start.1 = (bf16[128,2560]{1,0:T(8,128)(2,1)}, bf16[128,2560]{1,0:T(8,128)(2,1)}, u32[]{:S(2)}, u32[]{:S(2)}) collective-permute-start(bf16[128,2560]{1,0:T(8,128)(2,1)} %fusion.2), channel_id=1, source_target_pairs={{0,128},{128,256},{256,384},{1,129},{129,257},{257,385},{2,130},{1... | collective-permute-start | bytes 1966088 | tf_op jit(solution)/shard_map/ppermute | solution.py:272
  12.0 1.5 broadcast_in_dim.8
  13.5 15.3 %all-to-all-start = ((bf16[16,80,128]{2,1,0:T(8,128)(2,1)}), bf16[16,80,128]{2,1,0:T(8,128)(2,1)}, u32[]{:S(2)}, u32[]{:S(2)}) async-start(bf16[16,80,128]{2,1,0:T(8,128)(2,1)} %broadcast_in_dim.8), calls=%async_computation | async-start | bytes 655360 | tf_op jit(solution)/shard_map/all_to_all | solution.py:289
  28.9 0.0 collective-permute-done.1
  28.9 2.3 %fusion = bf16[128,2560]{1,0:T(8,128)(2,1)} fusion(bf16[128,2560]{1,0:T(8,128)(2,1)} %collective-permute-done.1, bf16[128,2560]{1,0:T(8,128)(2,1)} %fusion.2), kind=kLoop, calls=%fused_computation.5 | loop fusion | flops 1310720 | bytes 1966080 | tf_op jit(solution)/shard_map/convert_element_type | solution.py:278
  31.2 4.8 %collective-permute-start.2 = (bf16[128,2560]{1,0:T(8,128)(2,1)}, bf16[128,2560]{1,0:T(8,128)(2,1)}, u32[]{:S(2)}, u32[]{:S(2)}) collective-permute-start(bf16[128,2560]{1,0:T(8,128)(2,1)} %fusion), channel_id=1, source_target_pairs={{0,256},{128,384},{1,257},{129,385},{2,258},{130,386},{3,259},{131... | collective-permute-start | bytes 1966088 | tf_op jit(solution)/shard_map/ppermute | solution.py:279
  36.0 0.1 pad_add_fusion.place
  36.1 0.0 copy-done
  36.1 0.0 copy-done.4
  36.1 5.9 %deal_blocks.1 = (bf16[128,7168]{1,0:T(8,128)(2,1)S(1)}, bf16[64,7168]{1,0:T(8,128)(2,1)}, bf16[64,7168]{1,0:T(8,128)(2,1)}, s32[128]{0:T(128)S(1)}, s32[4]{0:T(128)S(1)}) custom-call(s32[4]{0:T(128)S(1)} %pad_add_fusion.place, s32[64]{0:T(128)S(1)} %copy-done.4, bf16[1,2,64,13824]{3,2,1,0:T(8,128)(2,1)S(1)} %copy-done), custom_call_target="tpu_custom_call" | custom-call | tf_op jit(solution)/shard_map/deal_blocks/pallas_call | solution.py:111
  42.0 0.0 copy-start.1
  42.0 1.3 copy-done.1
  43.3 2.0 %collective-permute-start.7 = (bf16[64,7168]{1,0:T(8,128)(2,1)}, bf16[64,7168]{1,0:T(8,128)(2,1)S(1)}, u32[]{:S(2)}, u32[]{:S(2)}) collective-permute-start(bf16[64,7168]{1,0:T(8,128)(2,1)} %get-tuple-element.17), channel_id=1, source_target_pairs={{0,1},{2,3},{4,5},{6,7},{8,9},{10,11},{12,13},{14,15},{1,0},{3,2},... | collective-permute-start | bytes 2752520 | tf_op jit(solution)/shard_map/ppermute | solution.py:258
  45.3 0.0 copy-done.5
  45.4 0.0 copy-done.6
  45.4 4.7 %collective-permute-start.8 = (bf16[64,7168]{1,0:T(8,128)(2,1)}, bf16[64,7168]{1,0:T(8,128)(2,1)S(1)}, u32[]{:S(2)}, u32[]{:S(2)}) collective-permute-start(bf16[64,7168]{1,0:T(8,128)(2,1)} %get-tuple-element.18), channel_id=1, source_target_pairs={{1,2},{3,4},{5,6},{7,8},{9,10},{11,12},{13,14},{15,0},{2,1},{4,3},... | collective-permute-start | bytes 2752520 | tf_op jit(solution)/shard_map/ppermute | solution.py:258
  50.1 0.0 all-to-all-done
  50.1 4.7 %collective-permute-start.6 = (bf16[1280,128]{1,0:T(8,128)(2,1)}, bf16[1280,128]{1,0:T(8,128)(2,1)S(1)}, u32[]{:S(2)}, u32[]{:S(2)}) collective-permute-start(bf16[1280,128]{1,0:T(8,128)(2,1)} %bitcast.6.refs_0_), channel_id=1, source_target_pairs={{0,48},{16,0},{32,16},{48,32},{1,49},{17,1},{33,17},{49,33},{2,50}... | collective-permute-start | bytes 983048 | tf_op jit(solution)/shard_map/ppermute | solution.py:263
  54.7 2.7 %collective-permute-start.5 = (bf16[1280,128]{1,0:T(8,128)(2,1)}, bf16[1280,128]{1,0:T(8,128)(2,1)S(1)}, u32[]{:S(2)}, u32[]{:S(2)}) collective-permute-start(bf16[1280,128]{1,0:T(8,128)(2,1)} %bitcast.6.refs_0_), channel_id=1, source_target_pairs={{0,32},{16,48},{32,0},{48,16},{1,33},{17,49},{33,1},{49,17},{2,34}... | collective-permute-start | bytes 983048 | tf_op jit(solution)/shard_map/ppermute | solution.py:263
  57.5 0.0 collective-permute-done.2
  57.5 2.8 %collective-permute-start.4 = (bf16[1280,128]{1,0:T(8,128)(2,1)}, bf16[1280,128]{1,0:T(8,128)(2,1)S(1)}, u32[]{:S(2)}, u32[]{:S(2)}) collective-permute-start(bf16[1280,128]{1,0:T(8,128)(2,1)} %bitcast.6.refs_0_), channel_id=1, source_target_pairs={{0,16},{16,32},{32,48},{48,0},{1,17},{17,33},{33,49},{49,1},{2,18}... | collective-permute-start | bytes 983048 | tf_op jit(solution)/shard_map/ppermute | solution.py:263
  60.3 2.2 %broadcast_select_fusion = (bf16[128,2560]{1,0:T(8,128)(2,1)S(1)}, bf16[128,2560]{1,0:T(8,128)(2,1)S(1)}, bf16[128,2560]{1,0:T(8,128)(2,1)S(1)}) fusion(pred[]{:T(512)S(6)} %eq.4, bf16[128,2560]{1,0:T(8,128)(2,1)} %collective-permute-done, bf16[128,5120]{1,0:T(8,128)(2,1)} %bitcast.9, s32[]{:T(128)S(6)} %select_n.37, ...), kind=kLoop, calls=%fused_computation.11 | loop fusion | flops 3932160 | bytes 4587525 | tf_op jit(solution)/shard_map/jit(_where)/select_n | solution.py:283
  62.5 5.2 %collective-permute-done.6.refs_3_ = bf16[1280,128]{1,0:T(8,128)(2,1)S(1)} collective-permute-done((bf16[1280,128]{1,0:T(8,128)(2,1)}, bf16[1280,128]{1,0:T(8,128)(2,1)S(1)}, u32[]{:S(2)}, u32[]{:S(2)}) %collective-permute-start.6) | collective-permute-done | bytes 327712 | tf_op jit(solution)/shard_map/ppermute | solution.py:263
  67.7 1.9 %collective-permute-start.3 = (bf16[128,2560]{1,0:T(8,128)(2,1)S(1)}, bf16[128,2560]{1,0:T(8,128)(2,1)S(1)}, u32[]{:S(2)}, u32[]{:S(2)}) collective-permute-start(bf16[128,2560]{1,0:T(8,128)(2,1)S(1)} %get-tuple-element.23), channel_id=1, source_target_pairs={{0,64},{64,0},{1,65},{65,1},{2,66},{66,2},{3,67},{67,3},{4,68},{68... | collective-permute-start | bytes 1966088 | tf_op jit(solution)/shard_map/ppermute | solution.py:263
  69.6 0.1 broadcast_select_fusion.1.mine
  69.7 0.0 collective-permute-done.5.refs_2_
  69.7 3.5 %collective-permute-done.4.refs_1_ = bf16[1280,128]{1,0:T(8,128)(2,1)S(1)} collective-permute-done((bf16[1280,128]{1,0:T(8,128)(2,1)}, bf16[1280,128]{1,0:T(8,128)(2,1)S(1)}, u32[]{:S(2)}, u32[]{:S(2)}) %collective-permute-start.4) | collective-permute-done | bytes 327712 | tf_op jit(solution)/shard_map/ppermute | solution.py:263
  73.2 0.0 collective-permute-done.3.other
  73.2 0.0 copy-done.3
  73.2 1.6 rotate.1.refs_0_
  74.8 0.0 collective-permute-done.7.refs_4_
  74.8 0.0 collective-permute-done.8.refs_5_
  74.8 2.2 %collective-permute-start.10 = (bf16[128,128]{1,0:T(8,128)(2,1)S(1)}, bf16[128,128]{1,0:T(8,128)(2,1)S(1)}, u32[]{:S(2)}, u32[]{:S(2)}) collective-permute-start(bf16[128,128]{1,0:T(8,128)(2,1)S(1)} %rotate.1.refs_0_), channel_id=1, source_target_pairs={{1,2},{3,4},{5,6},{7,8},{9,10},{11,12},{13,14},{15,0},{2,1},{4,3},... | collective-permute-start | bytes 98312 | tf_op jit(solution)/shard_map/ppermute | solution.py:258
  77.0 8.5 %collective-permute-start.9 = (bf16[128,128]{1,0:T(8,128)(2,1)S(1)}, bf16[128,128]{1,0:T(8,128)(2,1)S(1)}, u32[]{:S(2)}, u32[]{:S(2)}) collective-permute-start(bf16[128,128]{1,0:T(8,128)(2,1)S(1)} %rotate.1.refs_0_), channel_id=1, source_target_pairs={{0,1},{2,3},{4,5},{6,7},{8,9},{10,11},{12,13},{14,15},{1,0},{3,2},... | collective-permute-start | bytes 98312 | tf_op jit(solution)/shard_map/ppermute | solution.py:258
  85.6 0.0 collective-permute-done.10.refs_2_
  85.6 1.9 %collective-permute-done.9.refs_1_ = bf16[128,128]{1,0:T(8,128)(2,1)S(1)} collective-permute-done((bf16[128,128]{1,0:T(8,128)(2,1)S(1)}, bf16[128,128]{1,0:T(8,128)(2,1)S(1)}, u32[]{:S(2)}, u32[]{:S(2)}) %collective-permute-start.9) | collective-permute-done | bytes 32800 | tf_op jit(solution)/shard_map/ppermute | solution.py:258
  87.5 0.0 copy-done.2
  87.5 2.1 %square_sums.1 = bf16[8,7,128,128]{3,2,1,0:T(8,128)(2,1)S(1)} custom-call(bf16[128,128]{1,0:T(8,128)(2,1)S(1)} %rotate.1.refs_0_, bf16[128,128]{1,0:T(8,128)(2,1)S(1)} %collective-permute-done.9.refs_1_, bf16[128,128]{1,0:T(8,128)(2,1)S(1)} %collective-permute-done.10.refs_2_, bf16[128,7168]{1,0:T(8,128)(2,1)S(1)} %copy-done.2, ...), custom_call_target="tpu_custom_call" | custom-call | tf_op jit(solution)/shard_map/square_sums/pallas_call | solution.py:144
  89.6 26.8 %all_to_all.20.got = bf16[8,7,128,128]{3,2,1,0:T(8,128)(2,1)} all-to-all(bf16[8,7,128,128]{3,2,1,0:T(8,128)(2,1)S(1)} %square_sums.1), channel_id=1, replica_groups={{0,2,16,18,32,34,48,50},{1,3,17,19,33,35,49,51},{4,6,20,22,36,38,52,54}..., dimensions={0} | all-to-all | bytes 3670016 | tf_op jit(solution)/shard_map/all_to_all | solution.py:252
  116.3 2.6 %group_sums.1 = bf16[16,128,128]{2,1,0:T(8,128)(2,1)} custom-call(s32[4]{0:T(128)} %copy-done.3, s32[128]{0:T(128)} %copy-done.6, bf16[8,7,128,128]{3,2,1,0:T(8,128)(2,1)} %all_to_all.20.got), custom_call_target="tpu_custom_call" | custom-call | tf_op jit(solution)/shard_map/group_sums/pallas_call | solution.py:170
  119.0 40.9 %all_to_all.21.got = bf16[16,128,128]{2,1,0:T(8,128)(2,1)} all-to-all(bf16[16,128,128]{2,1,0:T(8,128)(2,1)} %group_sums.1), channel_id=1, replica_groups=mesh['y'=4,'c'=2,'x'=4,'z'=16] {'z'}, dimensions={0} | all-to-all | bytes 1048576 | tf_op jit(solution)/shard_map/all_to_all | solution.py:299
  159.8 1.9 %gather_nodes.1 = f32[4,128,128]{2,1,0:T(8,128)} custom-call(s32[4]{0:T(128)} %copy-done.3, s32[64]{0:T(128)} %counts.5, s32[4]{0:T(128)} %copy-done.5, bf16[16,128,128]{2,1,0:T(8,128)(2,1)} %all_to_all.21.got), custom_call_target="tpu_custom_call" | custom-call | tf_op jit(solution)/shard_map/gather_nodes/pallas_call | solution.py:200
  161.7 10.8 %all_to_all.22.got = f32[4,128,128]{2,1,0:T(8,128)} all-to-all(f32[4,128,128]{2,1,0:T(8,128)} %gather_nodes.1), channel_id=1, replica_groups=mesh['y'=4,'c'=2,'x'=4,'z'=16] {'x'}, dimensions={0} | all-to-all | bytes 524288 | tf_op jit(solution)/shard_map/all_to_all | solution.py:300
  172.5 1.8 %finish.1 = f32[1,4,128,128]{3,2,1,0:T(8,128)} custom-call(s32[4]{0:T(128)} %copy-done.3, s32[64]{0:T(128)} %counts.5, s32[4]{0:T(128)} %copy-done.5, f32[4,128,128]{2,1,0:T(8,128)} %all_to_all.22.got), custom_call_target="tpu_custom_call" | custom-call | tf_op jit(solution)/shard_map/finish/pallas_call | solution.py:227
  (6 shorter events, 0.0 us)
Async XLA Ops:
  1.1 4.1 %collective-permute-start = (bf16[128,2560]{1,0:T(8,128)(2,1)S(1)}, bf16[128,2560]{1,0:T(8,128)(2,1)}, u32[]{:S(2)}, u32[]{:S(2)}) collective-permute-start(bf16[128,2560]{1,0:T(8,128)(2,1)S(1)} %constant_dynamic-slice_fusion), channel_id=1, source_target_pairs={{0,64},{64,0},{1,65},{65,1},{2,66},{66,2},{3,67},{67,3},{4,68},{68... | collective-permute-start | bytes 1966088 | tf_op jit(solution)/shard_map/ppermute | solution.py:263
  5.3 30.8 %copy-start = (bf16[1,2,64,13824]{3,2,1,0:T(8,128)(2,1)S(1)}, bf16[1,2,64,13824]{3,2,1,0:T(8,128)(2,1)}, u32[]{:S(2)}) copy-start(bf16[1,2,64,13824]{3,2,1,0:T(8,128)(2,1)} %outgrad.1) | copy-start | bytes 10616836
  7.7 21.2 %collective-permute-start.1 = (bf16[128,2560]{1,0:T(8,128)(2,1)}, bf16[128,2560]{1,0:T(8,128)(2,1)}, u32[]{:S(2)}, u32[]{:S(2)}) collective-permute-start(bf16[128,2560]{1,0:T(8,128)(2,1)} %fusion.2), channel_id=1, source_target_pairs={{0,128},{128,256},{256,384},{1,129},{129,257},{257,385},{2,130},{1... | collective-permute-start | bytes 1966088 | tf_op jit(solution)/shard_map/ppermute | solution.py:272
  13.5 22.6 %copy-start.4 = (s32[64]{0:T(128)S(1)}, s32[64]{0:T(128)}, u32[]{:S(2)}) copy-start(s32[64]{0:T(128)} %counts.5) | copy-start | bytes 772
  13.5 36.5 %all-to-all-start = ((bf16[16,80,128]{2,1,0:T(8,128)(2,1)}), bf16[16,80,128]{2,1,0:T(8,128)(2,1)}, u32[]{:S(2)}, u32[]{:S(2)}) async-start(bf16[16,80,128]{2,1,0:T(8,128)(2,1)} %broadcast_in_dim.8), calls=%async_computation | async-start | bytes 655360 | tf_op jit(solution)/shard_map/all_to_all | solution.py:289
  31.2 26.3 %collective-permute-start.2 = (bf16[128,2560]{1,0:T(8,128)(2,1)}, bf16[128,2560]{1,0:T(8,128)(2,1)}, u32[]{:S(2)}, u32[]{:S(2)}) collective-permute-start(bf16[128,2560]{1,0:T(8,128)(2,1)} %fusion), channel_id=1, source_target_pairs={{0,256},{128,384},{1,257},{129,385},{2,258},{130,386},{3,259},{131... | collective-permute-start | bytes 1966088 | tf_op jit(solution)/shard_map/ppermute | solution.py:279
  36.1 37.1 %copy-start.3 = (s32[4]{0:T(128)}, s32[4]{0:T(128)S(1)}, u32[]{:S(2)}) copy-start(s32[4]{0:T(128)S(1)} %pad_add_fusion.place) | copy-start | bytes 52
  42.0 1.3 copy-start.1
  43.3 2.1 %copy-start.5 = (s32[4]{0:T(128)}, s32[4]{0:T(128)S(1)}, u32[]{:S(2)}) copy-start(s32[4]{0:T(128)S(1)} %get-tuple-element.14.starts) | copy-start | bytes 52
  43.3 2.1 %copy-start.6 = (s32[128]{0:T(128)}, s32[128]{0:T(128)S(1)}, u32[]{:S(2)}) copy-start(s32[128]{0:T(128)S(1)} %get-tuple-element.15.column_of) | copy-start | bytes 1540
  43.3 31.5 %collective-permute-start.7 = (bf16[64,7168]{1,0:T(8,128)(2,1)}, bf16[64,7168]{1,0:T(8,128)(2,1)S(1)}, u32[]{:S(2)}, u32[]{:S(2)}) collective-permute-start(bf16[64,7168]{1,0:T(8,128)(2,1)} %get-tuple-element.17), channel_id=1, source_target_pairs={{0,1},{2,3},{4,5},{6,7},{8,9},{10,11},{12,13},{14,15},{1,0},{3,2},... | collective-permute-start | bytes 2752520 | tf_op jit(solution)/shard_map/ppermute | solution.py:258
  45.4 29.5 %collective-permute-start.8 = (bf16[64,7168]{1,0:T(8,128)(2,1)}, bf16[64,7168]{1,0:T(8,128)(2,1)S(1)}, u32[]{:S(2)}, u32[]{:S(2)}) collective-permute-start(bf16[64,7168]{1,0:T(8,128)(2,1)} %get-tuple-element.18), channel_id=1, source_target_pairs={{1,2},{3,4},{5,6},{7,8},{9,10},{11,12},{13,14},{15,0},{2,1},{4,3},... | collective-permute-start | bytes 2752520 | tf_op jit(solution)/shard_map/ppermute | solution.py:258
  50.1 17.6 %collective-permute-start.6 = (bf16[1280,128]{1,0:T(8,128)(2,1)}, bf16[1280,128]{1,0:T(8,128)(2,1)S(1)}, u32[]{:S(2)}, u32[]{:S(2)}) collective-permute-start(bf16[1280,128]{1,0:T(8,128)(2,1)} %bitcast.6.refs_0_), channel_id=1, source_target_pairs={{0,48},{16,0},{32,16},{48,32},{1,49},{17,1},{33,17},{49,33},{2,50}... | collective-permute-start | bytes 983048 | tf_op jit(solution)/shard_map/ppermute | solution.py:263
  54.7 14.9 %collective-permute-start.5 = (bf16[1280,128]{1,0:T(8,128)(2,1)}, bf16[1280,128]{1,0:T(8,128)(2,1)S(1)}, u32[]{:S(2)}, u32[]{:S(2)}) collective-permute-start(bf16[1280,128]{1,0:T(8,128)(2,1)} %bitcast.6.refs_0_), channel_id=1, source_target_pairs={{0,32},{16,48},{32,0},{48,16},{1,33},{17,49},{33,1},{49,17},{2,34}... | collective-permute-start | bytes 983048 | tf_op jit(solution)/shard_map/ppermute | solution.py:263
  57.5 15.7 %collective-permute-start.4 = (bf16[1280,128]{1,0:T(8,128)(2,1)}, bf16[1280,128]{1,0:T(8,128)(2,1)S(1)}, u32[]{:S(2)}, u32[]{:S(2)}) collective-permute-start(bf16[1280,128]{1,0:T(8,128)(2,1)} %bitcast.6.refs_0_), channel_id=1, source_target_pairs={{0,16},{16,32},{32,48},{48,0},{1,17},{17,33},{33,49},{49,1},{2,18}... | collective-permute-start | bytes 983048 | tf_op jit(solution)/shard_map/ppermute | solution.py:263
  67.7 5.5 %collective-permute-start.3 = (bf16[128,2560]{1,0:T(8,128)(2,1)S(1)}, bf16[128,2560]{1,0:T(8,128)(2,1)S(1)}, u32[]{:S(2)}, u32[]{:S(2)}) collective-permute-start(bf16[128,2560]{1,0:T(8,128)(2,1)S(1)} %get-tuple-element.23), channel_id=1, source_target_pairs={{0,64},{64,0},{1,65},{65,1},{2,66},{66,2},{3,67},{67,3},{4,68},{68... | collective-permute-start | bytes 1966088 | tf_op jit(solution)/shard_map/ppermute | solution.py:263
  69.7 17.8 %copy-start.2 = (bf16[128,7168]{1,0:T(8,128)(2,1)S(1)}, bf16[128,7168]{1,0:T(8,128)(2,1)}, u32[]{:S(2)}) copy-start(bf16[128,7168]{1,0:T(8,128)(2,1)} %copy-done.1) | copy-start | bytes 5505028
  74.8 10.8 %collective-permute-start.10 = (bf16[128,128]{1,0:T(8,128)(2,1)S(1)}, bf16[128,128]{1,0:T(8,128)(2,1)S(1)}, u32[]{:S(2)}, u32[]{:S(2)}) collective-permute-start(bf16[128,128]{1,0:T(8,128)(2,1)S(1)} %rotate.1.refs_0_), channel_id=1, source_target_pairs={{1,2},{3,4},{5,6},{7,8},{9,10},{11,12},{13,14},{15,0},{2,1},{4,3},... | collective-permute-start | bytes 98312 | tf_op jit(solution)/shard_map/ppermute | solution.py:258
  77.0 10.4 %collective-permute-start.9 = (bf16[128,128]{1,0:T(8,128)(2,1)S(1)}, bf16[128,128]{1,0:T(8,128)(2,1)S(1)}, u32[]{:S(2)}, u32[]{:S(2)}) collective-permute-start(bf16[128,128]{1,0:T(8,128)(2,1)S(1)} %rotate.1.refs_0_), channel_id=1, source_target_pairs={{0,1},{2,3},{4,5},{6,7},{8,9},{10,11},{12,13},{14,15},{1,0},{3,2},... | collective-permute-start | bytes 98312 | tf_op jit(solution)/shard_map/ppermute | solution.py:258

commit v3 on v2

--- a/solution.py
+++ b/solution.py
@@ -64,21 +64,14 @@
     )(place, mine, other, *bases)
 
 
-def deal_kernel(place, counts, outgrad, kept, sent_up, sent_down, column_of, starts, offsets, block_of):
+def deal_kernel(place, counts, outgrad, kept, sent, column_of, starts, offsets, block_of):
     z = place[1]
 
     def prefix(o, run):
         offsets[o] = run
         return run + counts[o]
 
-    lax.fori_loop(0, N_X * N_Z, prefix, jnp.int32(0))
-
-    def fill(i, _):
-        column_of[i] = N_Z
-        block_of[i] = 0
-        return 0
-
-    lax.fori_loop(0, 128, fill, 0)
+    lax.fori_loop(0, N_X * N_Z, prefix, jnp.int32(0), unroll=8)
 
     def owner(i, g):
         column = i // N_X
@@ -88,31 +81,31 @@
         def _():
             starts[lax.rem(i, N_X)] = g
 
-        def block(s, _):
-            block_of[g + s] = offsets[o] + s
+        for s in range(CAP):
+            block_of[g + s] = jnp.minimum(offsets[o] + s, NBLK - 1)
             column_of[g + s] = column
-            return 0
-
-        lax.fori_loop(0, counts[o], block, 0)
         return g + counts[o]
 
-    lax.fori_loop(0, N_X * N_Z, owner, jnp.int32(0))
-    for m in range(2):
+    lax.fori_loop(0, N_X * N_Z, owner, jnp.int32(0), unroll=4)
+    for g in range(NBLK, 128):
+        column_of[g] = N_Z
+        block_of[g] = 0
+    for m, out in enumerate((kept, sent)):
         near = lax.rem(place[3] + m, 2)
         for i in range(SLOTS):
             g = 16 * (i // 8) + 8 * (i // 4 % 2) + 4 * near + i % 4
             lane = pl.multiple_of(block_of[g] * BLK, BLK)
             for n in range(2):
-                out = (kept.at[n * SEQ_LEN : (n + 1) * SEQ_LEN], (sent_up, sent_down)[n])[m]
-                out[:, i * BLK : (i + 1) * BLK] = outgrad[0, n, :, pl.ds(lane, BLK)]
+                rows = slice(n * SEQ_LEN, (n + 1) * SEQ_LEN)
+                out[rows, i * BLK : (i + 1) * BLK] = outgrad[0, n, :, pl.ds(lane, BLK)]
 
 
 def deal(place, counts, outgrad):
     return pl.pallas_call(
         deal_kernel,
-        out_shape=[sds((rows, WID), jnp.bfloat16) for rows in (TOK, SEQ_LEN, SEQ_LEN)] + [sds((128,), jnp.int32), sds((N_X,), jnp.int32)],
+        out_shape=[sds((TOK, WID), jnp.bfloat16)] * 2 + [sds((128,), jnp.int32), sds((N_X,), jnp.int32)],
         in_specs=[SMEM, SMEM, VMEM],
-        out_specs=[VMEM, VMEM, VMEM, SMEM, SMEM],
+        out_specs=[VMEM, VMEM, SMEM, SMEM],
         scratch_shapes=[pltpu.SMEM((N_X * N_Z,), jnp.int32), pltpu.SMEM((128,), jnp.int32)],
         compiler_params=pltpu.CompilerParams(vmem_limit_bytes=32 * 2**20),
         name="deal_blocks",
@@ -120,21 +113,20 @@
 
 
 def square_kernel(*refs):
-    (own, up, down), (kept, got_up, got_down) = refs[:3], refs[3:6]
-    out, lhs = refs[6:]
+    rots, grads = refs[:2], refs[2:4]
+    out, lhs = refs[4:]
     lane = lax.broadcasted_iota(jnp.int32, (EIG, TOK), 1)
     zero = jnp.zeros((EIG, TOK), jnp.bfloat16)
-    lhs[:EIG, :] = jnp.where(lane < SEQ_LEN, own[...], zero)
-    lhs[EIG:, :] = jnp.where(lane < SEQ_LEN, zero, own[...])
-    first, second = up[:, :SEQ_LEN], down[:, SEQ_LEN:]
+    for m in range(2):
+        lhs[m, :EIG, :] = jnp.where(lane < SEQ_LEN, rots[m][...], zero)
+        lhs[m, EIG:, :] = jnp.where(lane < SEQ_LEN, zero, rots[m][...])
     for i in range(0, SLOTS, 2):
-        cols = slice(i * BLK, (i + 2) * BLK)
-        made = jnp.dot(lhs[...], kept[:, cols], preferred_element_type=jnp.float32)
-        made = made * made
-        total = made[:EIG] + made[EIG:]
-        for rot, grad in ((first, got_up), (second, got_down)):
-            made = jnp.dot(rot, grad[:, cols], preferred_element_type=jnp.float32)
-            total = total + made * made
+        total = None
+        for m in range(2):
+            made = jnp.dot(lhs[m], grads[m][:, i * BLK : (i + 2) * BLK], preferred_element_type=jnp.float32)
+            made = made * made
+            made = made[:EIG] + made[EIG:]
+            total = made if m == 0 else total + made
         for k in range(2):
             member = 2 * ((i + k) % 4) + (i + k) // 4 % 2
             out[member, i // 8] = total[:, k * BLK : (k + 1) * BLK].astype(out.dtype)
@@ -144,9 +136,9 @@
     return pl.pallas_call(
         square_kernel,
         out_shape=sds((GROUP, PER, EIG, BLK), jnp.bfloat16),
-        in_specs=[VMEM] * 6,
-        out_specs=VMEM,
-        scratch_shapes=[pltpu.VMEM((2 * EIG, TOK), jnp.bfloat16)],
+        in_specs=[VMEM] * 4,
+        out_specs=VMEM,
+        scratch_shapes=[pltpu.VMEM((2, 2 * EIG, TOK), jnp.bfloat16)],
         compiler_params=pltpu.CompilerParams(vmem_limit_bytes=32 * 2**20),
         name="square_sums",
     )(*rots, *grads)
@@ -252,10 +244,9 @@
     return lax.all_to_all(v, SECTION + DP, 0, 0, axis_index_groups=groups, tiled=True)
 
 
-def swap(v, first):
-    pairs = [(first + p, first + p + 1) for p in range(0, N_Z, 2)]
-    pairs += [(b, a) for a, b in pairs]
-    return lax.ppermute(v, "z", [(a % N_Z, b % N_Z) for a, b in pairs])
+def pass_on(v):
+    perm = [(c * N_Z + z, c * N_Z + (z + 1 - 2 * c) % N_Z) for c in range(2) for z in range(N_Z)]
+    return lax.ppermute(v, ("c", "z"), perm)
 
 
 def shift(v, axis, k):
@@ -288,14 +279,14 @@
     place = jnp.stack([x, z, core, (z + 2 * core) % 4]).astype(jnp.int32)
     line = lax.all_to_all(jnp.broadcast_to(basis, (N_Z,) + basis.shape[1:]), "z", 0, 0, tiled=True)
     line = line.reshape(PLANE, EIG)
-    kept, up, down, column_of, starts = deal(place, counts, outgrad)
+    kept, sent, column_of, starts = deal(place, counts, outgrad)
     mine, theirs, pair, one = chip_sums(update)
-    grads = [kept, swap(up, 0), swap(down, 1)]
+    grads = [kept, pass_on(sent)]
     bases = [shift(line, "x", dx) for dx in range(N_X)]
     mine, other = stream(mine, theirs, pair, one)
     rotated = rotate(place, mine, other, bases)
     rotated, grads = lax.optimization_barrier((rotated, grads))
-    got = group_exchange(square([rotated, swap(rotated, 0), swap(rotated, 1)], grads))
+    got = group_exchange(square([rotated, pass_on(rotated)], grads))
     got = lax.all_to_all(group_sums(place, column_of, got), "z", 0, 0, tiled=True)
     got = lax.all_to_all(gather_nodes(place, counts, starts, got), "x", 0, 0, tiled=True)
     return finish(place, counts, starts, got)

time: 175 us -> 168 us (0.960)
  starting transfers between devices: 56 us -> 43.8 us
  waiting for transfers between devices: 12.8 us -> 19.8 us
    ppermute x4 -> x2, starting transfers between devices: 17.5 us -> 5.28 us  [pass_on(): return lax.ppermute(v, ('c', 'z'), perm)]
    all_to_all x1, waiting for transfers between devices: 0.01 us -> 3.37 us  [per_device(): lax.all_to_all(jnp.broadcast_to(basis, (N_Z,) + basis.shape[1:]), 'z', 0,...]
    ppermute x4 -> x2, waiting for transfers between devices: 1.88 us -> 5.17 us  [pass_on(): return lax.ppermute(v, ('c', 'z'), perm)]
    pallas_call x1, Pallas kernels: 5.94 us -> 3.89 us  [deal(): pl.pallas_call(deal_kernel, out_shape=[sds((TOK, WID), jnp.bfloat16)] * 2...]
    all_to_all x1, blocking collectives: 40.9 us -> 38.8 us  [per_device(): lax.all_to_all(group_sums(place, column_of, got), 'z', 0, 0, tiled=True)]
  transfers between devices with their start and end apart: 12 -> 10, of which waited for: 4 -> 6; matrix products, arithmetic and copies ran while one was open for 4% -> 4% of each run, Pallas kernels for 4% -> 3%
where the time goes in v3:
time: 168 us; the launch traced here: 167 us
  blocking collectives  77.2 us (46%)
  starting transfers between devices  43.8 us (26%)
  waiting for transfers between devices  19.8 us (12%)
  Pallas kernels  14.2 us (8%)
  other arithmetic  7.05 us (4%)
  local copies, waits for them, and re-layouts  4.96 us (3%)
    all_to_all x1, blocking collectives, per_device(): lax.all_to_all(group_sums(place, column_of, got), 'z', 0, 0, tiled=True)  38.8 us
    all_to_all x1, blocking collectives, group_exchange(): lax.all_to_all(v, SECTION + DP, 0, 0, axis_index_groups=groups, tiled=True)  27.6 us
    all_to_all x1, starting transfers between devices, per_device(): lax.all_to_all(jnp.broadcast_to(basis, (N_Z,) + basis.shape[1:]), 'z', 0,...  15.3 us
    ppermute x5, starting transfers between devices, shift(): lax.ppermute(v, axis, [(i, (i + k) % n) for i in range(n)])  14 us
    ppermute x5, waiting for transfers between devices, shift(): lax.ppermute(v, axis, [(i, (i + k) % n) for i in range(n)])  11.3 us
    all_to_all x1, blocking collectives, per_device(): lax.all_to_all(gather_nodes(place, counts, starts, got), 'x', 0, 0, tiled...  10.8 us
    ppermute x2, starting transfers between devices, pass_on(): return lax.ppermute(v, ('c', 'z'), perm)  5.28 us
    ppermute x2, waiting for transfers between devices, pass_on(): return lax.ppermute(v, ('c', 'z'), perm)  5.17 us
  transfers between devices with their start and end apart: 10, of which 6 were waited for; matrix products, arithmetic and copies ran while one was open for 4% of the time, Pallas kernels for 3%

profile of v3, /device:TPU:32, one launch (start us, length us, event | category | flops | bytes accessed | tf_op | source)
XLA Modules:
  0.0 167.1 jit_solution(2765856280609804187)
XLA Ops:
  0.0 1.1 constant_dynamic-slice_fusion
  1.1 1.9 %collective-permute-start = (bf16[128,2560]{1,0:T(8,128)(2,1)S(1)}, bf16[128,2560]{1,0:T(8,128)(2,1)}, u32[]{:S(2)}, u32[]{:S(2)}) collective-permute-start(bf16[128,2560]{1,0:T(8,128)(2,1)S(1)} %constant_dynamic-slice_fusion), channel_id=1, source_target_pairs={{0,64},{64,0},{1,65},{65,1},{2,66},{66,2},{3,67},{67,3},{4,68},{68... | collective-permute-start | bytes 1966088 | tf_op jit(solution)/shard_map/ppermute | solution.py:254
  3.1 2.2 %collective-permute-done = bf16[128,2560]{1,0:T(8,128)(2,1)} collective-permute-done((bf16[128,2560]{1,0:T(8,128)(2,1)S(1)}, bf16[128,2560]{1,0:T(8,128)(2,1)}, u32[]{:S(2)}, u32[]{:S(2)}) %collective-permute-start) | collective-permute-done | bytes 655392 | tf_op jit(solution)/shard_map/ppermute | solution.py:254
  5.3 0.0 copy-start
  5.3 2.4 %fusion.2 = bf16[128,2560]{1,0:T(8,128)(2,1)} fusion(bf16[128,2560]{1,0:T(8,128)(2,1)} %collective-permute-done, bf16[128,5120]{1,0:T(8,128)(2,1)} %bitcast.8, s32[]{:T(128)S(6)} %select_n.37), kind=kLoop, calls=%fused_computation.7 | loop fusion | flops 1310720 | bytes 1966084 | tf_op jit(solution)/shard_map/convert_element_type | solution.py:262
  7.7 4.3 %collective-permute-start.1 = (bf16[128,2560]{1,0:T(8,128)(2,1)}, bf16[128,2560]{1,0:T(8,128)(2,1)}, u32[]{:S(2)}, u32[]{:S(2)}) collective-permute-start(bf16[128,2560]{1,0:T(8,128)(2,1)} %fusion.2), channel_id=1, source_target_pairs={{0,128},{128,256},{256,384},{1,129},{129,257},{257,385},{2,130},{1... | collective-permute-start | bytes 1966088 | tf_op jit(solution)/shard_map/ppermute | solution.py:263
  12.0 1.5 broadcast_in_dim.8
  13.5 0.0 copy-start.4
  13.5 15.3 %all-to-all-start = ((bf16[16,80,128]{2,1,0:T(8,128)(2,1)}), bf16[16,80,128]{2,1,0:T(8,128)(2,1)}, u32[]{:S(2)}, u32[]{:S(2)}) async-start(bf16[16,80,128]{2,1,0:T(8,128)(2,1)} %broadcast_in_dim.8), calls=%async_computation | async-start | bytes 655360 | tf_op jit(solution)/shard_map/all_to_all | solution.py:280
  28.9 0.0 collective-permute-done.1
  28.9 2.3 %fusion = bf16[128,2560]{1,0:T(8,128)(2,1)} fusion(bf16[128,2560]{1,0:T(8,128)(2,1)} %collective-permute-done.1, bf16[128,2560]{1,0:T(8,128)(2,1)} %fusion.2), kind=kLoop, calls=%fused_computation.5 | loop fusion | flops 1310720 | bytes 1966080 | tf_op jit(solution)/shard_map/convert_element_type | solution.py:269
  31.2 4.8 %collective-permute-start.2 = (bf16[128,2560]{1,0:T(8,128)(2,1)}, bf16[128,2560]{1,0:T(8,128)(2,1)}, u32[]{:S(2)}, u32[]{:S(2)}) collective-permute-start(bf16[128,2560]{1,0:T(8,128)(2,1)} %fusion), channel_id=1, source_target_pairs={{0,256},{128,384},{1,257},{129,385},{2,258},{130,386},{3,259},{131... | collective-permute-start | bytes 1966088 | tf_op jit(solution)/shard_map/ppermute | solution.py:270
  36.0 0.1 pad_add_fusion.place
  36.1 0.0 copy-done
  36.1 0.0 copy-done.4
  36.1 0.0 copy-start.3
  36.1 3.9 %deal_blocks.1 = (bf16[128,7168]{1,0:T(8,128)(2,1)S(1)}, bf16[128,7168]{1,0:T(8,128)(2,1)}, s32[128]{0:T(128)S(1)}, s32[4]{0:T(128)S(1)}) custom-call(s32[4]{0:T(128)S(1)} %pad_add_fusion.place, s32[64]{0:T(128)S(1)} %copy-done.4, bf16[1,2,64,13824]{3,2,1,0:T(8,128)(2,1)S(1)} %copy-done), custom_call_target="tpu_custom_call" | custom-call | tf_op jit(solution)/shard_map/deal_blocks/pallas_call | solution.py:104
  40.0 0.0 copy-start.1
  40.0 1.2 copy-done.1
  41.2 0.6 copy-done.5
  41.8 0.5 copy-done.6
  42.3 3.4 %collective-permute-start.7 = (bf16[128,7168]{1,0:T(8,128)(2,1)}, bf16[128,7168]{1,0:T(8,128)(2,1)S(1)}, u32[]{:S(2)}, u32[]{:S(2)}) collective-permute-start(bf16[128,7168]{1,0:T(8,128)(2,1)} %get-tuple-element.15), channel_id=1, source_target_pairs={{0,1},{1,2},{2,3},{3,4},{4,5},{5,6},{6,7},{7,8},{8,9},{9,10},{10,1... | collective-permute-start | bytes 5505032 | tf_op jit(solution)/shard_map/ppermute | solution.py:249
  45.7 3.4 %all-to-all-done = bf16[16,80,128]{2,1,0:T(8,128)(2,1)} async-done(((bf16[16,80,128]{2,1,0:T(8,128)(2,1)}), bf16[16,80,128]{2,1,0:T(8,128)(2,1)}, u32[]{:S(2)}, u32[]{:S(2)}) %all-to-all-start) | async-done | bytes 327712 | tf_op jit(solution)/shard_map/all_to_all | solution.py:280
  49.0 4.7 %collective-permute-start.6 = (bf16[1280,128]{1,0:T(8,128)(2,1)}, bf16[1280,128]{1,0:T(8,128)(2,1)S(1)}, u32[]{:S(2)}, u32[]{:S(2)}) collective-permute-start(bf16[1280,128]{1,0:T(8,128)(2,1)} %bitcast.6.refs_0_), channel_id=1, source_target_pairs={{0,48},{16,0},{32,16},{48,32},{1,49},{17,1},{33,17},{49,33},{2,50}... | collective-permute-start | bytes 983048 | tf_op jit(solution)/shard_map/ppermute | solution.py:254
  53.7 2.7 %collective-permute-start.5 = (bf16[1280,128]{1,0:T(8,128)(2,1)}, bf16[1280,128]{1,0:T(8,128)(2,1)S(1)}, u32[]{:S(2)}, u32[]{:S(2)}) collective-permute-start(bf16[1280,128]{1,0:T(8,128)(2,1)} %bitcast.6.refs_0_), channel_id=1, source_target_pairs={{0,32},{16,48},{32,0},{48,16},{1,33},{17,49},{33,1},{49,17},{2,34}... | collective-permute-start | bytes 983048 | tf_op jit(solution)/shard_map/ppermute | solution.py:254
  56.4 2.8 %collective-permute-start.4 = (bf16[1280,128]{1,0:T(8,128)(2,1)}, bf16[1280,128]{1,0:T(8,128)(2,1)S(1)}, u32[]{:S(2)}, u32[]{:S(2)}) collective-permute-start(bf16[1280,128]{1,0:T(8,128)(2,1)} %bitcast.6.refs_0_), channel_id=1, source_target_pairs={{0,16},{16,32},{32,48},{48,0},{1,17},{17,33},{33,49},{49,1},{2,18}... | collective-permute-start | bytes 983048 | tf_op jit(solution)/shard_map/ppermute | solution.py:254
  59.2 0.0 collective-permute-done.2
  59.2 2.2 %broadcast_select_fusion = (bf16[128,2560]{1,0:T(8,128)(2,1)S(1)}, bf16[128,2560]{1,0:T(8,128)(2,1)S(1)}, bf16[128,2560]{1,0:T(8,128)(2,1)S(1)}) fusion(pred[]{:T(512)S(6)} %eq.4, bf16[128,2560]{1,0:T(8,128)(2,1)} %collective-permute-done, bf16[128,5120]{1,0:T(8,128)(2,1)} %bitcast.9, s32[]{:T(128)S(6)} %select_n.37, ...), kind=kLoop, calls=%fused_computation.11 | loop fusion | flops 3932160 | bytes 4587525 | tf_op jit(solution)/shard_map/jit(_where)/select_n | solution.py:274
  61.4 1.9 %collective-permute-start.3 = (bf16[128,2560]{1,0:T(8,128)(2,1)S(1)}, bf16[128,2560]{1,0:T(8,128)(2,1)S(1)}, u32[]{:S(2)}, u32[]{:S(2)}) collective-permute-start(bf16[128,2560]{1,0:T(8,128)(2,1)S(1)} %get-tuple-element.19), channel_id=1, source_target_pairs={{0,64},{64,0},{1,65},{65,1},{2,66},{66,2},{3,67},{67,3},{4,68},{68... | collective-permute-start | bytes 1966088 | tf_op jit(solution)/shard_map/ppermute | solution.py:254
  63.3 0.1 broadcast_select_fusion.1.mine
  63.4 0.0 copy-start.2
  63.4 3.6 %collective-permute-done.6.refs_3_ = bf16[1280,128]{1,0:T(8,128)(2,1)S(1)} collective-permute-done((bf16[1280,128]{1,0:T(8,128)(2,1)}, bf16[1280,128]{1,0:T(8,128)(2,1)S(1)}, u32[]{:S(2)}, u32[]{:S(2)}) %collective-permute-start.6) | collective-permute-done | bytes 327712 | tf_op jit(solution)/shard_map/ppermute | solution.py:254
  67.0 1.0 collective-permute-done.5.refs_2_
  68.0 4.5 %collective-permute-done.4.refs_1_ = bf16[1280,128]{1,0:T(8,128)(2,1)S(1)} collective-permute-done((bf16[1280,128]{1,0:T(8,128)(2,1)}, bf16[1280,128]{1,0:T(8,128)(2,1)S(1)}, u32[]{:S(2)}, u32[]{:S(2)}) %collective-permute-start.4) | collective-permute-done | bytes 327712 | tf_op jit(solution)/shard_map/ppermute | solution.py:254
  72.5 0.0 collective-permute-done.3.other
  72.5 0.0 copy-done.3
  72.5 1.6 rotate.1.refs_0_
  74.1 0.0 collective-permute-done.7.refs_3_
  74.1 1.9 %collective-permute-start.8 = (bf16[128,128]{1,0:T(8,128)(2,1)S(1)}, bf16[128,128]{1,0:T(8,128)(2,1)S(1)}, u32[]{:S(2)}, u32[]{:S(2)}) collective-permute-start(bf16[128,128]{1,0:T(8,128)(2,1)S(1)} %rotate.1.refs_0_), channel_id=1, source_target_pairs={{0,1},{1,2},{2,3},{3,4},{4,5},{5,6},{6,7},{7,8},{8,9},{9,10},{10,1... | collective-permute-start | bytes 98312 | tf_op jit(solution)/shard_map/ppermute | solution.py:249
  76.1 5.2 %collective-permute-done.8.refs_1_ = bf16[128,128]{1,0:T(8,128)(2,1)S(1)} collective-permute-done((bf16[128,128]{1,0:T(8,128)(2,1)S(1)}, bf16[128,128]{1,0:T(8,128)(2,1)S(1)}, u32[]{:S(2)}, u32[]{:S(2)}) %collective-permute-start.8) | collective-permute-done | bytes 32800 | tf_op jit(solution)/shard_map/ppermute | solution.py:249
  81.2 0.0 copy-done.2
  81.2 2.1 %square_sums.1 = bf16[8,7,128,128]{3,2,1,0:T(8,128)(2,1)S(1)} custom-call(bf16[128,128]{1,0:T(8,128)(2,1)S(1)} %rotate.1.refs_0_, bf16[128,128]{1,0:T(8,128)(2,1)S(1)} %collective-permute-done.8.refs_1_, bf16[128,7168]{1,0:T(8,128)(2,1)S(1)} %copy-done.2, bf16[128,7168]{1,0:T(8,128)(2,1)S(1)} %collective-permute-done.7.refs_3_), custom_call_target="tpu_custom_call" | custom-call | tf_op jit(solution)/shard_map/square_sums/pallas_call | solution.py:136
  83.3 27.6 %all_to_all.20.got = bf16[8,7,128,128]{3,2,1,0:T(8,128)(2,1)} all-to-all(bf16[8,7,128,128]{3,2,1,0:T(8,128)(2,1)S(1)} %square_sums.1), channel_id=1, replica_groups={{0,2,16,18,32,34,48,50},{1,3,17,19,33,35,49,51},{4,6,20,22,36,38,52,54}..., dimensions={0} | all-to-all | bytes 3670016 | tf_op jit(solution)/shard_map/all_to_all | solution.py:244
  110.9 2.6 %group_sums.1 = bf16[16,128,128]{2,1,0:T(8,128)(2,1)} custom-call(s32[4]{0:T(128)} %copy-done.3, s32[128]{0:T(128)} %copy-done.6, bf16[8,7,128,128]{3,2,1,0:T(8,128)(2,1)} %all_to_all.20.got), custom_call_target="tpu_custom_call" | custom-call | tf_op jit(solution)/shard_map/group_sums/pallas_call | solution.py:162
  113.6 38.8 %all_to_all.21.got = bf16[16,128,128]{2,1,0:T(8,128)(2,1)} all-to-all(bf16[16,128,128]{2,1,0:T(8,128)(2,1)} %group_sums.1), channel_id=1, replica_groups=mesh['y'=4,'c'=2,'x'=4,'z'=16] {'z'}, dimensions={0} | all-to-all | bytes 1048576 | tf_op jit(solution)/shard_map/all_to_all | solution.py:290
  152.4 1.9 %gather_nodes.1 = f32[4,128,128]{2,1,0:T(8,128)} custom-call(s32[4]{0:T(128)} %copy-done.3, s32[64]{0:T(128)} %counts.5, s32[4]{0:T(128)} %copy-done.5, bf16[16,128,128]{2,1,0:T(8,128)(2,1)} %all_to_all.21.got), custom_call_target="tpu_custom_call" | custom-call | tf_op jit(solution)/shard_map/gather_nodes/pallas_call | solution.py:192
  154.3 10.8 %all_to_all.22.got = f32[4,128,128]{2,1,0:T(8,128)} all-to-all(f32[4,128,128]{2,1,0:T(8,128)} %gather_nodes.1), channel_id=1, replica_groups=mesh['y'=4,'c'=2,'x'=4,'z'=16] {'x'}, dimensions={0} | all-to-all | bytes 524288 | tf_op jit(solution)/shard_map/all_to_all | solution.py:291
  165.1 2.1 %finish.1 = f32[1,4,128,128]{3,2,1,0:T(8,128)} custom-call(s32[4]{0:T(128)} %copy-done.3, s32[64]{0:T(128)} %counts.5, s32[4]{0:T(128)} %copy-done.5, f32[4,128,128]{2,1,0:T(8,128)} %all_to_all.22.got), custom_call_target="tpu_custom_call" | custom-call | tf_op jit(solution)/shard_map/finish/pallas_call | solution.py:219
  (2 shorter events, 0.0 us)
Async XLA Ops:
  1.1 4.1 %collective-permute-start = (bf16[128,2560]{1,0:T(8,128)(2,1)S(1)}, bf16[128,2560]{1,0:T(8,128)(2,1)}, u32[]{:S(2)}, u32[]{:S(2)}) collective-permute-start(bf16[128,2560]{1,0:T(8,128)(2,1)S(1)} %constant_dynamic-slice_fusion), channel_id=1, source_target_pairs={{0,64},{64,0},{1,65},{65,1},{2,66},{66,2},{3,67},{67,3},{4,68},{68... | collective-permute-start | bytes 1966088 | tf_op jit(solution)/shard_map/ppermute | solution.py:254
  5.3 30.8 %copy-start = (bf16[1,2,64,13824]{3,2,1,0:T(8,128)(2,1)S(1)}, bf16[1,2,64,13824]{3,2,1,0:T(8,128)(2,1)}, u32[]{:S(2)}) copy-start(bf16[1,2,64,13824]{3,2,1,0:T(8,128)(2,1)} %outgrad.1) | copy-start | bytes 10616836
  7.7 21.2 %collective-permute-start.1 = (bf16[128,2560]{1,0:T(8,128)(2,1)}, bf16[128,2560]{1,0:T(8,128)(2,1)}, u32[]{:S(2)}, u32[]{:S(2)}) collective-permute-start(bf16[128,2560]{1,0:T(8,128)(2,1)} %fusion.2), channel_id=1, source_target_pairs={{0,128},{128,256},{256,384},{1,129},{129,257},{257,385},{2,130},{1... | collective-permute-start | bytes 1966088 | tf_op jit(solution)/shard_map/ppermute | solution.py:263
  13.5 22.5 %copy-start.4 = (s32[64]{0:T(128)S(1)}, s32[64]{0:T(128)}, u32[]{:S(2)}) copy-start(s32[64]{0:T(128)} %counts.5) | copy-start | bytes 772
  13.5 35.5 %all-to-all-start = ((bf16[16,80,128]{2,1,0:T(8,128)(2,1)}), bf16[16,80,128]{2,1,0:T(8,128)(2,1)}, u32[]{:S(2)}, u32[]{:S(2)}) async-start(bf16[16,80,128]{2,1,0:T(8,128)(2,1)} %broadcast_in_dim.8), calls=%async_computation | async-start | bytes 655360 | tf_op jit(solution)/shard_map/all_to_all | solution.py:280
  31.2 28.0 %collective-permute-start.2 = (bf16[128,2560]{1,0:T(8,128)(2,1)}, bf16[128,2560]{1,0:T(8,128)(2,1)}, u32[]{:S(2)}, u32[]{:S(2)}) collective-permute-start(bf16[128,2560]{1,0:T(8,128)(2,1)} %fusion), channel_id=1, source_target_pairs={{0,256},{128,384},{1,257},{129,385},{2,258},{130,386},{3,259},{131... | collective-permute-start | bytes 1966088 | tf_op jit(solution)/shard_map/ppermute | solution.py:270
  36.1 36.4 %copy-start.3 = (s32[4]{0:T(128)}, s32[4]{0:T(128)S(1)}, u32[]{:S(2)}) copy-start(s32[4]{0:T(128)S(1)} %pad_add_fusion.place) | copy-start | bytes 52
  40.0 1.2 copy-start.1
  41.2 0.6 copy-start.5
  41.8 0.5 copy-start.6
  42.3 31.8 %collective-permute-start.7 = (bf16[128,7168]{1,0:T(8,128)(2,1)}, bf16[128,7168]{1,0:T(8,128)(2,1)S(1)}, u32[]{:S(2)}, u32[]{:S(2)}) collective-permute-start(bf16[128,7168]{1,0:T(8,128)(2,1)} %get-tuple-element.15), channel_id=1, source_target_pairs={{0,1},{1,2},{2,3},{3,4},{4,5},{5,6},{6,7},{7,8},{8,9},{9,10},{10,1... | collective-permute-start | bytes 5505032 | tf_op jit(solution)/shard_map/ppermute | solution.py:249
  49.0 18.0 %collective-permute-start.6 = (bf16[1280,128]{1,0:T(8,128)(2,1)}, bf16[1280,128]{1,0:T(8,128)(2,1)S(1)}, u32[]{:S(2)}, u32[]{:S(2)}) collective-permute-start(bf16[1280,128]{1,0:T(8,128)(2,1)} %bitcast.6.refs_0_), channel_id=1, source_target_pairs={{0,48},{16,0},{32,16},{48,32},{1,49},{17,1},{33,17},{49,33},{2,50}... | collective-permute-start | bytes 983048 | tf_op jit(solution)/shard_map/ppermute | solution.py:254
  53.7 14.3 %collective-permute-start.5 = (bf16[1280,128]{1,0:T(8,128)(2,1)}, bf16[1280,128]{1,0:T(8,128)(2,1)S(1)}, u32[]{:S(2)}, u32[]{:S(2)}) collective-permute-start(bf16[1280,128]{1,0:T(8,128)(2,1)} %bitcast.6.refs_0_), channel_id=1, source_target_pairs={{0,32},{16,48},{32,0},{48,16},{1,33},{17,49},{33,1},{49,17},{2,34}... | collective-permute-start | bytes 983048 | tf_op jit(solution)/shard_map/ppermute | solution.py:254
  56.4 16.1 %collective-permute-start.4 = (bf16[1280,128]{1,0:T(8,128)(2,1)}, bf16[1280,128]{1,0:T(8,128)(2,1)S(1)}, u32[]{:S(2)}, u32[]{:S(2)}) collective-permute-start(bf16[1280,128]{1,0:T(8,128)(2,1)} %bitcast.6.refs_0_), channel_id=1, source_target_pairs={{0,16},{16,32},{32,48},{48,0},{1,17},{17,33},{33,49},{49,1},{2,18}... | collective-permute-start | bytes 983048 | tf_op jit(solution)/shard_map/ppermute | solution.py:254
  61.4 11.1 %collective-permute-start.3 = (bf16[128,2560]{1,0:T(8,128)(2,1)S(1)}, bf16[128,2560]{1,0:T(8,128)(2,1)S(1)}, u32[]{:S(2)}, u32[]{:S(2)}) collective-permute-start(bf16[128,2560]{1,0:T(8,128)(2,1)S(1)} %get-tuple-element.19), channel_id=1, source_target_pairs={{0,64},{64,0},{1,65},{65,1},{2,66},{66,2},{3,67},{67,3},{4,68},{68... | collective-permute-start | bytes 1966088 | tf_op jit(solution)/shard_map/ppermute | solution.py:254
  63.4 17.8 %copy-start.2 = (bf16[128,7168]{1,0:T(8,128)(2,1)S(1)}, bf16[128,7168]{1,0:T(8,128)(2,1)}, u32[]{:S(2)}) copy-start(bf16[128,7168]{1,0:T(8,128)(2,1)} %copy-done.1) | copy-start | bytes 5505028
  74.1 7.1 %collective-permute-start.8 = (bf16[128,128]{1,0:T(8,128)(2,1)S(1)}, bf16[128,128]{1,0:T(8,128)(2,1)S(1)}, u32[]{:S(2)}, u32[]{:S(2)}) collective-permute-start(bf16[128,128]{1,0:T(8,128)(2,1)S(1)} %rotate.1.refs_0_), channel_id=1, source_target_pairs={{0,1},{1,2},{2,3},{3,4},{4,5},{5,6},{6,7},{7,8},{8,9},{9,10},{10,1... | collective-permute-start | bytes 98312 | tf_op jit(solution)/shard_map/ppermute | solution.py:249

commit v4 on v3

--- a/solution.py
+++ b/solution.py
@@ -64,7 +64,7 @@
     )(place, mine, other, *bases)
 
 
-def deal_kernel(place, counts, outgrad, kept, sent, column_of, starts, offsets, block_of):
+def deal_kernel(place, counts, outgrad, kept, sent, column_of, offsets, block_of):
     z = place[1]
 
     def prefix(o, run):
@@ -79,7 +79,7 @@
 
         @pl.when(column == z)
         def _():
-            starts[lax.rem(i, N_X)] = g
+            column_of[128 + lax.rem(i, N_X)] = g
 
         for s in range(CAP):
             block_of[g + s] = jnp.minimum(offsets[o] + s, NBLK - 1)
@@ -103,9 +103,9 @@
 def deal(place, counts, outgrad):
     return pl.pallas_call(
         deal_kernel,
-        out_shape=[sds((TOK, WID), jnp.bfloat16)] * 2 + [sds((128,), jnp.int32), sds((N_X,), jnp.int32)],
+        out_shape=[sds((TOK, WID), jnp.bfloat16)] * 2 + [sds((256,), jnp.int32)],
         in_specs=[SMEM, SMEM, VMEM],
-        out_specs=[VMEM, VMEM, SMEM, SMEM],
+        out_specs=[VMEM, VMEM, SMEM],
         scratch_shapes=[pltpu.SMEM((N_X * N_Z,), jnp.int32), pltpu.SMEM((128,), jnp.int32)],
         compiler_params=pltpu.CompilerParams(vmem_limit_bytes=32 * 2**20),
         name="deal_blocks",
@@ -146,7 +146,6 @@
 
 def group_kernel(place, column_of, got, out):
     first = 4 * place[3] + place[0]
-    out[...] = jnp.zeros(out.shape, out.dtype)
     for j in range(PER):
         column = column_of[16 * j + first]
 
@@ -171,7 +170,7 @@
 def gather_kernel(place, counts, starts, got, out):
     x, z, core = place[0], place[1], place[2]
     for k in range(N_X):
-        start = starts[k]
+        start = starts[128 + k]
         g = start + mod(x - start + 128, N_X)
         member = lax.rem(g // 4 + 2 * core, 4)
         owned = g < start + counts[k * N_Z + z]
@@ -200,7 +199,7 @@
 
 def finish_kernel(place, counts, starts, got, out):
     x, z = place[0], place[1]
-    start = starts[x]
+    start = starts[128 + x]
     owned = counts[x * N_Z + z]
     scale = 1.0 / (SEQ_LEN * SEQ_LEN * SEQS)
     for s in range(CAP):
@@ -259,15 +258,14 @@
     own = update[0].reshape(TOK, D)
     mine = lax.dynamic_slice_in_dim(own, core * (D // 2), D // 2, 1)
     theirs = shift(lax.dynamic_slice_in_dim(own, (1 - core) * (D // 2), D // 2, 1), "c", 1)
-    pair = (mine.astype(jnp.float32) + theirs.astype(jnp.float32)).astype(jnp.bfloat16)
-    return mine, theirs, pair, lax.ppermute(pair, "y", [(0, 1), (1, 2), (2, 3)])
-
-
-def stream(mine, theirs, pair, one):
+    return mine, theirs, (mine.astype(jnp.float32) + theirs.astype(jnp.float32)).astype(jnp.bfloat16)
+
+
+def stream(mine, theirs, pair):
     core = lax.axis_index("c")
     mine, theirs = mine.astype(jnp.float32), theirs.astype(jnp.float32)
-    two = (pair.astype(jnp.float32) + one.astype(jnp.float32)).astype(jnp.bfloat16)
-    before = one.astype(jnp.float32) + lax.ppermute(two, "y", [(0, 2), (1, 3)]).astype(jnp.float32)
+    steps = [lax.ppermute(pair, "y", [(i, i + k) for i in range(4 - k)]) for k in range(1, 4)]
+    before = steps[0].astype(jnp.float32) + steps[1].astype(jnp.float32) + steps[2].astype(jnp.float32)
     low = before + jnp.where(core == 0, mine, theirs)
     high = low + jnp.where(core == 0, theirs, mine)
     low, high = low.astype(jnp.bfloat16), high.astype(jnp.bfloat16)
@@ -279,17 +277,17 @@
     place = jnp.stack([x, z, core, (z + 2 * core) % 4]).astype(jnp.int32)
     line = lax.all_to_all(jnp.broadcast_to(basis, (N_Z,) + basis.shape[1:]), "z", 0, 0, tiled=True)
     line = line.reshape(PLANE, EIG)
-    kept, sent, column_of, starts = deal(place, counts, outgrad)
-    mine, theirs, pair, one = chip_sums(update)
+    kept, sent, table = deal(place, counts, outgrad)
+    mine, theirs, pair = chip_sums(update)
     grads = [kept, pass_on(sent)]
     bases = [shift(line, "x", dx) for dx in range(N_X)]
-    mine, other = stream(mine, theirs, pair, one)
+    mine, other = stream(mine, theirs, pair)
     rotated = rotate(place, mine, other, bases)
     rotated, grads = lax.optimization_barrier((rotated, grads))
     got = group_exchange(square([rotated, pass_on(rotated)], grads))
-    got = lax.all_to_all(group_sums(place, column_of, got), "z", 0, 0, tiled=True)
-    got = lax.all_to_all(gather_nodes(place, counts, starts, got), "x", 0, 0, tiled=True)
-    return finish(place, counts, starts, got)
+    got = lax.all_to_all(group_sums(place, table, got), "z", 0, 0, tiled=True)
+    got = lax.all_to_all(gather_nodes(place, counts, table, got), "x", 0, 0, tiled=True)
+    return finish(place, counts, table, got)
 
 
 def solution(mesh):

time: 168 us -> 166 us (0.988)
  the two profiles are of different devices: /device:TPU:32 before, /device:TPU:16 now
where the time goes in v4:
time: 166 us
  blocking collectives  78.1 us (47%)
  starting transfers between devices  43.5 us (26%)
  waiting for transfers between devices  20.4 us (12%)
  Pallas kernels  13.9 us (8%)
  other arithmetic  4.91 us (3%)
  local copies, waits for them, and re-layouts  4.64 us (3%)
    all_to_all x1, blocking collectives, per_device(): got = lax.all_to_all(group_sums(place, table, got), 'z', 0, 0, tiled=True)  36.2 us
    all_to_all x1, blocking collectives, group_exchange(): lax.all_to_all(v, SECTION + DP, 0, 0, axis_index_groups=groups, tiled=True)  31.1 us
    all_to_all x1, starting transfers between devices, per_device(): lax.all_to_all(jnp.broadcast_to(basis, (N_Z,) + basis.shape[1:]), 'z', 0,...  15.4 us
    ppermute x5, starting transfers between devices, shift(): lax.ppermute(v, axis, [(i, (i + k) % n) for i in range(n)])  15.2 us
    all_to_all x1, blocking collectives, per_device(): lax.all_to_all(gather_nodes(place, counts, table, got), 'x', 0, 0, tiled=...  10.8 us
    ppermute x3, waiting for transfers between devices, stream(): lax.ppermute(pair, 'y', [(i, i + k) for i in range(4 - k)])  10.4 us
    ppermute x2, starting transfers between devices, pass_on(): return lax.ppermute(v, ('c', 'z'), perm)  6.96 us
    ppermute x3, starting transfers between devices, stream(): lax.ppermute(pair, 'y', [(i, i + k) for i in range(4 - k)])  6 us
  transfers between devices with their start and end apart: 11, of which 4 were waited for; matrix products, arithmetic and copies ran while one was open for 3% of the time, Pallas kernels for 3%

profile of v4, /device:TPU:16, one launch (start us, length us, event | category | flops | bytes accessed | tf_op | source)
XLA Modules:
  0.0 165.6 jit_solution(1759923471814371856)
XLA Ops:
  0.0 0.0 copy-start.6
  0.0 0.0 copy-start
  0.0 2.1 %constant_dynamic-slice_fusion = bf16[128,2560]{1,0:T(8,128)(2,1)} fusion(bf16[128,5120]{1,0:T(8,128)(2,1)} %bitcast.7, s32[]{:T(128)S(6)} %select_n.38), kind=kLoop, calls=%fused_computation.11 | loop fusion | bytes 1310724 | tf_op jit(solution)/shard_map/dynamic_slice | solution.py:260
  2.1 1.9 %collective-permute-start = (bf16[128,2560]{1,0:T(8,128)(2,1)}, bf16[128,2560]{1,0:T(8,128)(2,1)}, u32[]{:S(2)}, u32[]{:S(2)}) collective-permute-start(bf16[128,2560]{1,0:T(8,128)(2,1)} %constant_dynamic-slice_fusion), channel_id=1, source_target_pairs={{0,64},{64,0},{1,65},{65,1},{2,66},{66,2},{3,67},{67,3},{4,68},{68... | collective-permute-start | bytes 1966088 | tf_op jit(solution)/shard_map/ppermute | solution.py:253
  4.0 0.0 copy-done.6
  4.1 0.8 broadcast_in_dim.8
  4.8 15.4 %all-to-all-start = ((bf16[16,80,128]{2,1,0:T(8,128)(2,1)}), bf16[16,80,128]{2,1,0:T(8,128)(2,1)}, u32[]{:S(2)}, u32[]{:S(2)}) async-start(bf16[16,80,128]{2,1,0:T(8,128)(2,1)} %broadcast_in_dim.8), calls=%async_computation | async-start | bytes 655360 | tf_op jit(solution)/shard_map/all_to_all | solution.py:278
  20.2 0.0 collective-permute-done
  20.2 2.3 %fusion = bf16[128,2560]{1,0:T(8,128)(2,1)} fusion(bf16[128,2560]{1,0:T(8,128)(2,1)} %collective-permute-done, bf16[128,5120]{1,0:T(8,128)(2,1)} %bitcast.8, s32[]{:T(128)S(6)} %select_n.37), kind=kLoop, calls=%fused_computation.3 | loop fusion | flops 1310720 | bytes 1966084 | tf_op jit(solution)/shard_map/convert_element_type | solution.py:261
  22.5 3.2 %collective-permute-start.1 = (bf16[128,2560]{1,0:T(8,128)(2,1)}, bf16[128,2560]{1,0:T(8,128)(2,1)}, u32[]{:S(2)}, u32[]{:S(2)}) collective-permute-start(bf16[128,2560]{1,0:T(8,128)(2,1)} %fusion), channel_id=1, source_target_pairs={{0,128},{128,256},{256,384},{1,129},{129,257},{257,385},{2,130},{1... | collective-permute-start | bytes 1966088 | tf_op jit(solution)/shard_map/ppermute | solution.py:267
  25.7 1.3 collective-permute-start.2
  27.0 1.5 collective-permute-start.3
  28.5 0.1 pad_add_fusion.place
  28.6 0.0 copy-done
  28.6 0.0 copy-done.5
  28.6 3.9 %deal_blocks.1 = (bf16[128,7168]{1,0:T(8,128)(2,1)S(1)}, bf16[128,7168]{1,0:T(8,128)(2,1)}, s32[256]{0:T(256)S(1)}) custom-call(s32[4]{0:T(128)S(1)} %pad_add_fusion.place, s32[64]{0:T(128)S(1)} %copy-done.5, bf16[1,2,64,13824]{3,2,1,0:T(8,128)(2,1)S(1)} %copy-done), custom_call_target="tpu_custom_call" | custom-call | tf_op jit(solution)/shard_map/deal_blocks/pallas_call | solution.py:104
  32.5 0.0 copy-start.1
  32.5 1.2 copy-done.1
  33.7 0.5 copy-done.4
  34.3 3.8 %collective-permute-start.8 = (bf16[128,7168]{1,0:T(8,128)(2,1)}, bf16[128,7168]{1,0:T(8,128)(2,1)S(1)}, u32[]{:S(2)}, u32[]{:S(2)}) collective-permute-start(bf16[128,7168]{1,0:T(8,128)(2,1)} %get-tuple-element.13), channel_id=1, source_target_pairs={{0,1},{1,2},{2,3},{3,4},{4,5},{5,6},{6,7},{7,8},{8,9},{9,10},{10,1... | collective-permute-start | bytes 5505032 | tf_op jit(solution)/shard_map/ppermute | solution.py:248
  38.1 3.8 %all-to-all-done = bf16[16,80,128]{2,1,0:T(8,128)(2,1)} async-done(((bf16[16,80,128]{2,1,0:T(8,128)(2,1)}), bf16[16,80,128]{2,1,0:T(8,128)(2,1)}, u32[]{:S(2)}, u32[]{:S(2)}) %all-to-all-start) | async-done | bytes 327712 | tf_op jit(solution)/shard_map/all_to_all | solution.py:278
  41.8 3.4 %collective-permute-start.5 = (bf16[1280,128]{1,0:T(8,128)(2,1)}, bf16[1280,128]{1,0:T(8,128)(2,1)S(1)}, u32[]{:S(2)}, u32[]{:S(2)}) collective-permute-start(bf16[1280,128]{1,0:T(8,128)(2,1)} %bitcast.6.refs_0_), channel_id=1, source_target_pairs={{0,16},{16,32},{32,48},{48,0},{1,17},{17,33},{33,49},{49,1},{2,18}... | collective-permute-start | bytes 983048 | tf_op jit(solution)/shard_map/ppermute | solution.py:253
  45.2 10.4 %collective-permute-done.1 = bf16[128,2560]{1,0:T(8,128)(2,1)} collective-permute-done((bf16[128,2560]{1,0:T(8,128)(2,1)}, bf16[128,2560]{1,0:T(8,128)(2,1)}, u32[]{:S(2)}, u32[]{:S(2)}) %collective-permute-start.1) | collective-permute-done | bytes 655392 | tf_op jit(solution)/shard_map/ppermute | solution.py:267
  55.6 4.9 %collective-permute-start.6 = (bf16[1280,128]{1,0:T(8,128)(2,1)}, bf16[1280,128]{1,0:T(8,128)(2,1)S(1)}, u32[]{:S(2)}, u32[]{:S(2)}) collective-permute-start(bf16[1280,128]{1,0:T(8,128)(2,1)} %bitcast.6.refs_0_), channel_id=1, source_target_pairs={{0,32},{16,48},{32,0},{48,16},{1,33},{17,49},{33,1},{49,17},{2,34}... | collective-permute-start | bytes 983048 | tf_op jit(solution)/shard_map/ppermute | solution.py:253
  60.5 0.0 collective-permute-done.2
  60.5 3.0 %collective-permute-start.7 = (bf16[1280,128]{1,0:T(8,128)(2,1)}, bf16[1280,128]{1,0:T(8,128)(2,1)S(1)}, u32[]{:S(2)}, u32[]{:S(2)}) collective-permute-start(bf16[1280,128]{1,0:T(8,128)(2,1)} %bitcast.6.refs_0_), channel_id=1, source_target_pairs={{0,48},{16,0},{32,16},{48,32},{1,49},{17,1},{33,17},{49,33},{2,50}... | collective-permute-start | bytes 983048 | tf_op jit(solution)/shard_map/ppermute | solution.py:253
  63.6 0.0 collective-permute-done.3
  63.6 2.5 %broadcast_select_fusion = (bf16[128,2560]{1,0:T(8,128)(2,1)S(1)}, bf16[128,2560]{1,0:T(8,128)(2,1)S(1)}, bf16[128,2560]{1,0:T(8,128)(2,1)S(1)}) fusion(pred[]{:T(512)S(6)} %eq.4, bf16[128,2560]{1,0:T(8,128)(2,1)} %collective-permute-done, bf16[128,5120]{1,0:T(8,128)(2,1)} %bitcast.9, s32[]{:T(128)S(6)} %select_n.37, ...), kind=kLoop, calls=%fused_computation.8 | loop fusion | flops 4587520 | bytes 5242885 | tf_op jit(solution)/shard_map/jit(_where)/select_n | solution.py:272
  66.1 1.9 %collective-permute-start.4 = (bf16[128,2560]{1,0:T(8,128)(2,1)S(1)}, bf16[128,2560]{1,0:T(8,128)(2,1)S(1)}, u32[]{:S(2)}, u32[]{:S(2)}) collective-permute-start(bf16[128,2560]{1,0:T(8,128)(2,1)S(1)} %get-tuple-element.17), channel_id=1, source_target_pairs={{0,64},{64,0},{1,65},{65,1},{2,66},{66,2},{3,67},{67,3},{4,68},{68... | collective-permute-start | bytes 1966088 | tf_op jit(solution)/shard_map/ppermute | solution.py:253
  68.0 0.1 broadcast_select_fusion.1.mine
  68.1 0.0 copy-start.2
  68.1 0.0 collective-permute-done.5.refs_1_
  68.1 0.0 collective-permute-done.6.refs_2_
  68.1 2.4 %collective-permute-done.7.refs_3_ = bf16[1280,128]{1,0:T(8,128)(2,1)S(1)} collective-permute-done((bf16[1280,128]{1,0:T(8,128)(2,1)}, bf16[1280,128]{1,0:T(8,128)(2,1)S(1)}, u32[]{:S(2)}, u32[]{:S(2)}) %collective-permute-start.7) | collective-permute-done | bytes 327712 | tf_op jit(solution)/shard_map/ppermute | solution.py:253
  70.5 0.0 collective-permute-done.4.other
  70.5 0.0 copy-done.3
  70.5 1.6 rotate.1.refs_0_
  72.2 0.0 collective-permute-done.8.refs_3_
  72.2 3.2 %collective-permute-start.9 = (bf16[128,128]{1,0:T(8,128)(2,1)S(1)}, bf16[128,128]{1,0:T(8,128)(2,1)S(1)}, u32[]{:S(2)}, u32[]{:S(2)}) collective-permute-start(bf16[128,128]{1,0:T(8,128)(2,1)S(1)} %rotate.1.refs_0_), channel_id=1, source_target_pairs={{0,1},{1,2},{2,3},{3,4},{4,5},{5,6},{6,7},{7,8},{8,9},{9,10},{10,1... | collective-permute-start | bytes 98312 | tf_op jit(solution)/shard_map/ppermute | solution.py:248
  75.4 3.8 %collective-permute-done.9.refs_1_ = bf16[128,128]{1,0:T(8,128)(2,1)S(1)} collective-permute-done((bf16[128,128]{1,0:T(8,128)(2,1)S(1)}, bf16[128,128]{1,0:T(8,128)(2,1)S(1)}, u32[]{:S(2)}, u32[]{:S(2)}) %collective-permute-start.9) | collective-permute-done | bytes 32800 | tf_op jit(solution)/shard_map/ppermute | solution.py:248
  79.2 0.0 copy-done.2
  79.2 2.1 %square_sums.1 = bf16[8,7,128,128]{3,2,1,0:T(8,128)(2,1)S(1)} custom-call(bf16[128,128]{1,0:T(8,128)(2,1)S(1)} %rotate.1.refs_0_, bf16[128,128]{1,0:T(8,128)(2,1)S(1)} %collective-permute-done.9.refs_1_, bf16[128,7168]{1,0:T(8,128)(2,1)S(1)} %copy-done.2, bf16[128,7168]{1,0:T(8,128)(2,1)S(1)} %collective-permute-done.8.refs_3_), custom_call_target="tpu_custom_call" | custom-call | tf_op jit(solution)/shard_map/square_sums/pallas_call | solution.py:136
  81.3 31.1 %all_to_all.20.got = bf16[8,7,128,128]{3,2,1,0:T(8,128)(2,1)} all-to-all(bf16[8,7,128,128]{3,2,1,0:T(8,128)(2,1)S(1)} %square_sums.1), channel_id=1, replica_groups={{0,2,16,18,32,34,48,50},{1,3,17,19,33,35,49,51},{4,6,20,22,36,38,52,54}..., dimensions={0} | all-to-all | bytes 3670016 | tf_op jit(solution)/shard_map/all_to_all | solution.py:243
  112.4 2.6 %group_sums.1 = bf16[16,128,128]{2,1,0:T(8,128)(2,1)} custom-call(s32[4]{0:T(128)} %copy-done.3, s32[256]{0:T(256)} %copy-done.4, bf16[8,7,128,128]{3,2,1,0:T(8,128)(2,1)} %all_to_all.20.got), custom_call_target="tpu_custom_call" | custom-call | tf_op jit(solution)/shard_map/group_sums/pallas_call | solution.py:161
  115.0 36.2 %all_to_all.21.got = bf16[16,128,128]{2,1,0:T(8,128)(2,1)} all-to-all(bf16[16,128,128]{2,1,0:T(8,128)(2,1)} %group_sums.1), channel_id=1, replica_groups=mesh['y'=4,'c'=2,'x'=4,'z'=16] {'z'}, dimensions={0} | all-to-all | bytes 1048576 | tf_op jit(solution)/shard_map/all_to_all | solution.py:288
  151.2 1.9 %gather_nodes.1 = f32[4,128,128]{2,1,0:T(8,128)} custom-call(s32[4]{0:T(128)} %copy-done.3, s32[64]{0:T(128)} %counts.5, s32[256]{0:T(256)} %copy-done.4, bf16[16,128,128]{2,1,0:T(8,128)(2,1)} %all_to_all.21.got), custom_call_target="tpu_custom_call" | custom-call | tf_op jit(solution)/shard_map/gather_nodes/pallas_call | solution.py:191
  153.1 10.8 %all_to_all.22.got = f32[4,128,128]{2,1,0:T(8,128)} all-to-all(f32[4,128,128]{2,1,0:T(8,128)} %gather_nodes.1), channel_id=1, replica_groups=mesh['y'=4,'c'=2,'x'=4,'z'=16] {'x'}, dimensions={0} | all-to-all | bytes 524288 | tf_op jit(solution)/shard_map/all_to_all | solution.py:289
  163.8 1.8 %finish.1 = f32[1,4,128,128]{3,2,1,0:T(8,128)} custom-call(s32[4]{0:T(128)} %copy-done.3, s32[64]{0:T(128)} %counts.5, s32[256]{0:T(256)} %copy-done.4, f32[4,128,128]{2,1,0:T(8,128)} %all_to_all.22.got), custom_call_target="tpu_custom_call" | custom-call | tf_op jit(solution)/shard_map/finish/pallas_call | solution.py:218
  (3 shorter events, 0.0 us)
Async XLA Ops:
  0.0 4.0 %copy-start.6 = (bf16[1,80,128]{2,1,0:T(8,128)(2,1)S(1)}, bf16[1,80,128]{2,1,0:T(8,128)(2,1)}, u32[]{:S(2)}) copy-start(bf16[1,80,128]{2,1,0:T(8,128)(2,1)} %param.6) | copy-start | bytes 61444
  0.0 28.6 %copy-start = (bf16[1,2,64,13824]{3,2,1,0:T(8,128)(2,1)S(1)}, bf16[1,2,64,13824]{3,2,1,0:T(8,128)(2,1)}, u32[]{:S(2)}) copy-start(bf16[1,2,64,13824]{3,2,1,0:T(8,128)(2,1)} %outgrad.1) | copy-start | bytes 10616836
  2.1 18.1 %collective-permute-start = (bf16[128,2560]{1,0:T(8,128)(2,1)}, bf16[128,2560]{1,0:T(8,128)(2,1)}, u32[]{:S(2)}, u32[]{:S(2)}) collective-permute-start(bf16[128,2560]{1,0:T(8,128)(2,1)} %constant_dynamic-slice_fusion), channel_id=1, source_target_pairs={{0,64},{64,0},{1,65},{65,1},{2,66},{66,2},{3,67},{67,3},{4,68},{68... | collective-permute-start | bytes 1966088 | tf_op jit(solution)/shard_map/ppermute | solution.py:253
  4.8 23.8 %copy-start.5 = (s32[64]{0:T(128)S(1)}, s32[64]{0:T(128)}, u32[]{:S(2)}) copy-start(s32[64]{0:T(128)} %counts.5) | copy-start | bytes 772
  4.8 37.0 %all-to-all-start = ((bf16[16,80,128]{2,1,0:T(8,128)(2,1)}), bf16[16,80,128]{2,1,0:T(8,128)(2,1)}, u32[]{:S(2)}, u32[]{:S(2)}) async-start(bf16[16,80,128]{2,1,0:T(8,128)(2,1)} %broadcast_in_dim.8), calls=%async_computation | async-start | bytes 655360 | tf_op jit(solution)/shard_map/all_to_all | solution.py:278
  22.5 33.1 %collective-permute-start.1 = (bf16[128,2560]{1,0:T(8,128)(2,1)}, bf16[128,2560]{1,0:T(8,128)(2,1)}, u32[]{:S(2)}, u32[]{:S(2)}) collective-permute-start(bf16[128,2560]{1,0:T(8,128)(2,1)} %fusion), channel_id=1, source_target_pairs={{0,128},{128,256},{256,384},{1,129},{129,257},{257,385},{2,130},{1... | collective-permute-start | bytes 1966088 | tf_op jit(solution)/shard_map/ppermute | solution.py:267
  25.7 34.8 %collective-permute-start.2 = (bf16[128,2560]{1,0:T(8,128)(2,1)}, bf16[128,2560]{1,0:T(8,128)(2,1)}, u32[]{:S(2)}, u32[]{:S(2)}) collective-permute-start(bf16[128,2560]{1,0:T(8,128)(2,1)} %fusion), channel_id=1, source_target_pairs={{0,256},{128,384},{1,257},{129,385},{2,258},{130,386},{3,259},{131... | collective-permute-start | bytes 1966088 | tf_op jit(solution)/shard_map/ppermute | solution.py:267
  27.0 36.6 %collective-permute-start.3 = (bf16[128,2560]{1,0:T(8,128)(2,1)}, bf16[128,2560]{1,0:T(8,128)(2,1)}, u32[]{:S(2)}, u32[]{:S(2)}) collective-permute-start(bf16[128,2560]{1,0:T(8,128)(2,1)} %fusion), channel_id=1, source_target_pairs={{0,384},{1,385},{2,386},{3,387},{4,388},{5,389},{6,390},{7,391},{8... | collective-permute-start | bytes 1966088 | tf_op jit(solution)/shard_map/ppermute | solution.py:267
  28.6 41.9 %copy-start.3 = (s32[4]{0:T(128)}, s32[4]{0:T(128)S(1)}, u32[]{:S(2)}) copy-start(s32[4]{0:T(128)S(1)} %pad_add_fusion.place) | copy-start | bytes 52
  32.5 1.2 copy-start.1
  33.7 0.5 copy-start.4
  34.3 37.9 %collective-permute-start.8 = (bf16[128,7168]{1,0:T(8,128)(2,1)}, bf16[128,7168]{1,0:T(8,128)(2,1)S(1)}, u32[]{:S(2)}, u32[]{:S(2)}) collective-permute-start(bf16[128,7168]{1,0:T(8,128)(2,1)} %get-tuple-element.13), channel_id=1, source_target_pairs={{0,1},{1,2},{2,3},{3,4},{4,5},{5,6},{6,7},{7,8},{8,9},{9,10},{10,1... | collective-permute-start | bytes 5505032 | tf_op jit(solution)/shard_map/ppermute | solution.py:248
  41.8 26.3 %collective-permute-start.5 = (bf16[1280,128]{1,0:T(8,128)(2,1)}, bf16[1280,128]{1,0:T(8,128)(2,1)S(1)}, u32[]{:S(2)}, u32[]{:S(2)}) collective-permute-start(bf16[1280,128]{1,0:T(8,128)(2,1)} %bitcast.6.refs_0_), channel_id=1, source_target_pairs={{0,16},{16,32},{32,48},{48,0},{1,17},{17,33},{33,49},{49,1},{2,18}... | collective-permute-start | bytes 983048 | tf_op jit(solution)/shard_map/ppermute | solution.py:253
  55.6 12.5 %collective-permute-start.6 = (bf16[1280,128]{1,0:T(8,128)(2,1)}, bf16[1280,128]{1,0:T(8,128)(2,1)S(1)}, u32[]{:S(2)}, u32[]{:S(2)}) collective-permute-start(bf16[1280,128]{1,0:T(8,128)(2,1)} %bitcast.6.refs_0_), channel_id=1, source_target_pairs={{0,32},{16,48},{32,0},{48,16},{1,33},{17,49},{33,1},{49,17},{2,34}... | collective-permute-start | bytes 983048 | tf_op jit(solution)/shard_map/ppermute | solution.py:253
  60.5 10.0 %collective-permute-start.7 = (bf16[1280,128]{1,0:T(8,128)(2,1)}, bf16[1280,128]{1,0:T(8,128)(2,1)S(1)}, u32[]{:S(2)}, u32[]{:S(2)}) collective-permute-start(bf16[1280,128]{1,0:T(8,128)(2,1)} %bitcast.6.refs_0_), channel_id=1, source_target_pairs={{0,48},{16,0},{32,16},{48,32},{1,49},{17,1},{33,17},{49,33},{2,50}... | collective-permute-start | bytes 983048 | tf_op jit(solution)/shard_map/ppermute | solution.py:253
  66.1 4.5 %collective-permute-start.4 = (bf16[128,2560]{1,0:T(8,128)(2,1)S(1)}, bf16[128,2560]{1,0:T(8,128)(2,1)S(1)}, u32[]{:S(2)}, u32[]{:S(2)}) collective-permute-start(bf16[128,2560]{1,0:T(8,128)(2,1)S(1)} %get-tuple-element.17), channel_id=1, source_target_pairs={{0,64},{64,0},{1,65},{65,1},{2,66},{66,2},{3,67},{67,3},{4,68},{68... | collective-permute-start | bytes 1966088 | tf_op jit(solution)/shard_map/ppermute | solution.py:253
  68.1 11.1 %copy-start.2 = (bf16[128,7168]{1,0:T(8,128)(2,1)S(1)}, bf16[128,7168]{1,0:T(8,128)(2,1)}, u32[]{:S(2)}) copy-start(bf16[128,7168]{1,0:T(8,128)(2,1)} %copy-done.1) | copy-start | bytes 5505028
  72.2 7.0 %collective-permute-start.9 = (bf16[128,128]{1,0:T(8,128)(2,1)S(1)}, bf16[128,128]{1,0:T(8,128)(2,1)S(1)}, u32[]{:S(2)}, u32[]{:S(2)}) collective-permute-start(bf16[128,128]{1,0:T(8,128)(2,1)S(1)} %rotate.1.refs_0_), channel_id=1, source_target_pairs={{0,1},{1,2},{2,3},{3,4},{4,5},{5,6},{6,7},{7,8},{8,9},{9,10},{10,1... | collective-permute-start | bytes 98312 | tf_op jit(solution)/shard_map/ppermute | solution.py:248
